TPU v7x, 256 devices: a whole 4x4x8 slice. The times are simulated.
256 devices in a mesh: gx: 4 (over x), gy: 4 (over z_lo), gz: 16 (over z_hi, y, core).
Axes of the slice: x: 4, y: 4, z: 8 (z_hi: 2, z_lo: 4; z = z_hi * 4 + z_lo), core: 2. Of those that a mesh axis runs over, the one named last changes fastest.
Arguments:
- fields: float32 [4, 64, 64, 2048], P(None, 'gx', 'gy', 'gz'), may hold values from -6 to 6
- tone_freq: float32 [48], replicated, may hold values from 0.02 to 2.5
- mode_freq: float32 [2000], replicated, may hold values from 0.05 to 2.5
- mode_amp: float32 [2000], replicated, may hold values from -3 to 3
- mode_map: int32 [2000], replicated, may hold values from 0 to 47
- src_pos: int32 [3, 4096], replicated, may hold values from 16 to 1535, as said below
- src_id: int32 [4096], replicated, may hold values from 0 to 47
- src_gain: float32 [4096], replicated, may hold values from -6 to 6
- sample_cell: int32 [4, 4, 16, 16, 128], P('gx', 'gy', 'gz'), may hold values from 0 to 32767
- sample_count: int32 [4, 4, 16, 16], P('gx', 'gy', None, 'gz'), may hold values from 0 to 128, as said below
- history: float32 [124, 4, 4, 16, 16, 128], P(None, 'gx', 'gy', 'gz'), may hold values from -6 to 6
Outputs:
- fields_out: float32 [4, 64, 64, 2048], P(None, 'gx', 'gy', 'gz')
- coefficients: float32 [96, 4, 4, 16, 16, 128], P(None, 'gx', 'gy', 'gz')
Inputs may be any that keep to these rules, and one draw needn't show every extreme that they name: `src_pos`: row 0 is below 64, row 1 below 64, row 2 below 2048; the cells lie on the surface of a box inside the grid. `sample_count`: in every draw some owner receives 128 live slots from every tile of its column. `sample_cell`: slots at or past the count also hold cells of the tile.
All inputs are finite; a program needn't handle non-finite values.
Results may differ from a plain program's by a relative error of at most 0.00017.
Values sent between devices are 32-bit elements; how exact they have to be, the bound alone decides.
A program may use at most 128 MiB of HBM per device.

v0:
```python
import math

import jax
import jax.numpy as jnp
from jax import lax
from jax.sharding import PartitionSpec as P

STEPS = 4
HIST = 124
SOURCES = 48


COURANT = 0.5


def padded(block, sides, width):
    for axis, dim in sides:
        count = lax.axis_size(axis)
        forward = [(i, i + 1) for i in range(count - 1)]
        backward = [(target, source) for source, target in forward]
        low = lax.ppermute(
            lax.slice_in_dim(block, block.shape[dim] - width, None, axis=dim), axis, forward
        )
        high = lax.ppermute(lax.slice_in_dim(block, 0, width, axis=dim), axis, backward)
        block = jnp.concatenate([low, block, high], axis=dim)
    return block


def ahead_difference(values, direction):
    size_along = values.shape[direction]
    following = jnp.concatenate(
        [
            lax.slice_in_dim(values, 1, size_along, axis=direction),
            jnp.zeros_like(lax.slice_in_dim(values, 0, 1, axis=direction)),
        ],
        axis=direction,
    )
    return following - values


def behind_difference(values, direction):
    size_along = values.shape[direction]
    previous = jnp.concatenate(
        [
            jnp.zeros_like(lax.slice_in_dim(values, 0, 1, axis=direction)),
            lax.slice_in_dim(values, 0, size_along - 1, axis=direction),
        ],
        axis=direction,
    )
    return values - previous


def source_drive(mode_freq, mode_amp, mode_map):
    moments = (HIST + jnp.arange(STEPS)).astype(jnp.float32)
    selector = (mode_map[None, :] == jnp.arange(SOURCES)[:, None]).astype(jnp.float32)
    waves = mode_amp[:, None] * jnp.sin(mode_freq[:, None] * moments[None, :])
    return jnp.dot(selector, waves, precision=lax.Precision.HIGHEST)


def sine_basis(tone_freq):
    moments = jnp.arange(HIST + STEPS).astype(jnp.float32)
    angles = moments[:, None] * tone_freq[None, :]
    return jnp.concatenate([jnp.cos(angles), jnp.sin(angles)], axis=1)


def span_mask(anchor, length, extent, margin):
    positions = anchor - margin + jnp.arange(length + 2 * margin)
    return ((positions >= 0) & (positions < extent)).astype(jnp.float32)


def body(
    fields,
    tone_freq,
    mode_freq,
    mode_amp,
    mode_map,
    src_pos,
    src_id,
    src_gain,
    sample_cell,
    sample_count,
    history,
):
    tile_x, tile_y, tile_z = (fields.shape[1], fields.shape[2], fields.shape[3])
    owners = lax.axis_size("gz")
    anchor_x = lax.axis_index("gx") * tile_x
    anchor_y = lax.axis_index("gy") * tile_y
    anchor_z = lax.axis_index("gz") * tile_z
    extent_x = tile_x * lax.axis_size("gx")
    extent_y = tile_y * lax.axis_size("gy")
    extent_z = tile_z * owners
    source_wave = source_drive(mode_freq, mode_amp, mode_map)
    selector = (src_id[:, None] == jnp.arange(SOURCES)[None, :]).astype(jnp.float32)
    cell_drive = src_gain[:, None] * jnp.dot(selector, source_wave, precision=lax.Precision.HIGHEST)
    margin = 1
    wide_x = tile_x + 2 * margin
    wide_y = tile_y + 2 * margin
    wide_z = tile_z + 2 * margin
    inside = (
        span_mask(anchor_x, tile_x, extent_x, margin)[:, None, None]
        * span_mask(anchor_y, tile_y, extent_y, margin)[None, :, None]
        * span_mask(anchor_z, tile_z, extent_z, margin)[None, None, :]
    )
    local_x = src_pos[0] - anchor_x + margin
    local_y = src_pos[1] - anchor_y + margin
    local_z = src_pos[2] - anchor_z + margin
    within = (
        (local_x >= 0)
        & (local_x < wide_x)
        & (local_y >= 0)
        & (local_y < wide_y)
        & (local_z >= 0)
        & (local_z < wide_z)
    ).astype(jnp.float32)
    source_flat = (
        jnp.clip(local_x, 0, wide_x - 1) * wide_y + jnp.clip(local_y, 0, wide_y - 1)
    ) * wide_z + jnp.clip(local_z, 0, wide_z - 1)
    source_weights = cell_drive * within[:, None]
    source_map = (
        jnp.zeros((wide_x * wide_y * wide_z, STEPS), jnp.float32)
        .at[source_flat]
        .add(source_weights)
    )
    sample_cells = sample_cell.reshape(owners, -1)
    sample_flat = (
        (
            (sample_cells // (tile_y * tile_z) + margin) * wide_y
            + sample_cells // tile_z % tile_y
            + margin
        )
        * wide_z
        + sample_cells % tile_z
        + margin
    )
    state_block = fields
    heard_list = []
    for opening in range(0, STEPS, margin):
        widened = padded(state_block, (("gx", 1), ("gy", 2), ("gz", 3)), 1)
        pressure, along_x, along_y, along_z = (widened[0], widened[1], widened[2], widened[3])
        along_x = (along_x - COURANT * ahead_difference(pressure, 0)) * inside
        along_y = (along_y - COURANT * ahead_difference(pressure, 1)) * inside
        along_z = (along_z - COURANT * ahead_difference(pressure, 2)) * inside
        pressure = (
            pressure
            - COURANT
            * (
                behind_difference(along_x, 0)
                + behind_difference(along_y, 1)
                + behind_difference(along_z, 2)
            )
        ) * inside
        pressure = pressure + source_map[:, opening].reshape(wide_x, wide_y, wide_z)
        sampled = pressure.reshape(-1)[sample_flat]
        heard_list.append(lax.all_to_all(sampled, "gz", split_axis=0, concat_axis=0, tiled=True))
        state_block = jnp.stack([pressure, along_x, along_y, along_z])[
            :, margin : margin + tile_x, margin : margin + tile_y, margin : margin + tile_z
        ]
    recorded = jnp.stack(heard_list)
    slots = sample_cell.shape[4]
    timeline = jnp.concatenate([history.reshape(HIST, -1), recorded.reshape(STEPS, -1)], axis=0)
    basis = sine_basis(tone_freq)
    coefficients = jnp.dot(basis.T, timeline, precision=lax.Precision.HIGHEST) * math.sqrt(
        2.0 / (HIST + STEPS)
    )
    occupied = (
        (jnp.arange(slots)[None, :] < sample_count.reshape(owners)[:, None])
        .astype(jnp.float32)
        .reshape(-1)
    )
    coefficients = coefficients * occupied[None, :]
    return (state_block, coefficients.reshape(basis.shape[1], 1, 1, 1, owners, slots))


def solution(mesh):
    in_specs = (
        P(None, "gx", "gy", "gz"),
        P(),
        P(),
        P(),
        P(),
        P(),
        P(),
        P(),
        P("gx", "gy", "gz", None, None),
        P("gx", "gy", None, "gz"),
        P(None, "gx", "gy", "gz", None, None),
    )
    out_specs = (P(None, "gx", "gy", "gz"), P(None, "gx", "gy", "gz", None, None))
    return jax.shard_map(body, mesh=mesh, in_specs=in_specs, out_specs=out_specs, check_vma=False)
```

profile of v0, /device:TPU:1, one launch (start us, length us, event | category | flops | bytes accessed | tf_op | source)
XLA Modules:
  0.0 367.4 jit_solution(14247795463770746272)
XLA Ops:
  1.4 3.9 %collective-permute-start = (f32[4,1,16,128]{3,2,1,0:T(8,128)S(1)}, f32[4,1,16,128]{3,2,1,0:T(8,128)S(1)}, u32[]{:S(2)}, u32[]{:S(2)}) collective-permute-start(f32[4,1,16,128]{3,2,1,0:T(8,128)S(1)} %get-tuple-element.53), channel_id=1, source_target_pairs={{0,64},{64,128},{128,192},{1,65},{65,129},{129,193},{2,66},{66,130... | collective-permute-start | bytes 98312 | tf_op jit(solution)/shard_map/ppermute | solution.py:21
  5.4 1.3 collective-permute-start.1
  8.8 1.3 fusion.21
  11.9 37.4 %scatter_custom_fusion = f32[42120,4]{1,0:T(8,128)} fusion(s32[4096]{0:T(1024)S(1)} %bitcast.236, f32[4096,4]{1,0:T(8,128)S(1)} %copy.58, f32[]{:T(128)} %constant.79.clone.1), kind=kCustom, calls=%fused_computation.9 | custom fusion | flops 16384 | bytes 673924 | tf_op jit(solution)/shard_map/scatter-add | solution.py:122
  49.2 49.8 %slice_reduce_fusion = (f32[42120]{0:T(1024)S(1)}, f32[42120]{0:T(1024)S(1)}, f32[42120]{0:T(1024)}, f32[42120]{0:T(1024)S(1)}) fusion(f32[42120,4]{1,0:T(8,128)} %scatter_custom_fusion), kind=kLoop, calls=%fused_computation.5 | loop fusion | bytes 1347840 | tf_op jit(solution)/shard_map/slice | solution.py:152
  99.1 1.3 collective-permute-start.3
  100.4 4.0 %collective-permute-start.2 = (f32[4,18,1,128]{3,2,1,0:T(1,128)S(1)}, f32[4,18,1,128]{3,2,1,0:T(1,128)S(1)}, u32[]{:S(2)}, u32[]{:S(2)}) collective-permute-start(f32[4,18,1,128]{3,2,1,0:T(1,128)S(1)} %get-tuple-element.50), channel_id=1, source_target_pairs={{0,16},{16,32},{32,48},{1,17},{17,33},{33,49},{2,18},{18,34},{34,5... | collective-permute-start | bytes 110600 | tf_op jit(solution)/shard_map/ppermute | solution.py:21
  106.5 4.0 %collective-permute-start.5 = (f32[4,18,18,1]{2,0,3,1:T(4,128)S(1)}, f32[4,18,18,1]{2,0,3,1:T(4,128)S(1)}, u32[]{:S(2)}, u32[]{:S(2)}) collective-permute-start(f32[4,18,18,1]{2,0,3,1:T(4,128)S(1)} %copy.55), channel_id=1, source_target_pairs={{1,0},{2,1},{3,2},{4,3},{5,4},{6,5},{7,6},{8,7},{9,8},{10,9},{11,1... | collective-permute-start | bytes 15560 | tf_op jit(solution)/shard_map/ppermute | solution.py:24
  111.0 3.1 collective-permute-start.4
  115.1 1.3 copy.56
  118.6 1.3 collective-permute-start.7
  119.9 4.0 %collective-permute-start.6 = (f32[4,1,16,128]{3,2,1,0:T(8,128)S(1)}, f32[4,1,16,128]{3,2,1,0:T(8,128)S(1)}, u32[]{:S(2)}, u32[]{:S(2)}) collective-permute-start(f32[4,1,16,128]{3,2,1,0:T(8,128)S(1)} %get-tuple-element.34), channel_id=1, source_target_pairs={{0,64},{64,128},{128,192},{1,65},{65,129},{129,193},{2,66},{66,130... | collective-permute-start | bytes 98312 | tf_op jit(solution)/shard_map/ppermute | solution.py:21
  124.9 1.3 collective-permute-start.9
  126.2 4.6 %collective-permute-start.8 = (f32[4,18,1,128]{3,2,1,0:T(1,128)S(1)}, f32[4,18,1,128]{3,2,1,0:T(1,128)S(1)}, u32[]{:S(2)}, u32[]{:S(2)}) collective-permute-start(f32[4,18,1,128]{3,2,1,0:T(1,128)S(1)} %get-tuple-element.48), channel_id=1, source_target_pairs={{0,16},{16,32},{32,48},{1,17},{17,33},{33,49},{2,18},{18,34},{34,5... | collective-permute-start | bytes 110600 | tf_op jit(solution)/shard_map/ppermute | solution.py:21
  134.0 3.6 collective-permute-start.11
  138.2 4.8 %collective-permute-start.10 = (f32[4,18,18,1]{2,0,3,1:T(4,128)S(1)}, f32[4,18,18,1]{2,0,3,1:T(4,128)}, u32[]{:S(2)}, u32[]{:S(2)}) collective-permute-start(f32[4,18,18,1]{2,0,3,1:T(4,128)S(1)} %copy.59), channel_id=1, source_target_pairs={{0,1},{1,2},{2,3},{3,4},{4,5},{5,6},{6,7},{7,8},{8,9},{9,10},{10,1... | collective-permute-start | bytes 15560 | tf_op jit(solution)/shard_map/ppermute | solution.py:21
  144.8 1.3 copy.61
  146.2 1.9 pad_maximum_fusion.1
  150.4 4.6 %collective-permute-start.12 = (f32[4,1,16,128]{3,2,1,0:T(8,128)S(1)}, f32[4,1,16,128]{3,2,1,0:T(8,128)S(1)}, u32[]{:S(2)}, u32[]{:S(2)}) collective-permute-start(f32[4,1,16,128]{3,2,1,0:T(8,128)S(1)} %get-tuple-element.32), channel_id=1, source_target_pairs={{0,64},{64,128},{128,192},{1,65},{65,129},{129,193},{2,66},{66,130... | collective-permute-start | bytes 98312 | tf_op jit(solution)/shard_map/ppermute | solution.py:21
  156.1 1.3 collective-permute-start.15
  157.4 4.6 %collective-permute-start.14 = (f32[4,18,1,128]{3,2,1,0:T(1,128)S(1)}, f32[4,18,1,128]{3,2,1,0:T(1,128)S(1)}, u32[]{:S(2)}, u32[]{:S(2)}) collective-permute-start(f32[4,18,1,128]{3,2,1,0:T(1,128)S(1)} %get-tuple-element.46), channel_id=1, source_target_pairs={{0,16},{16,32},{32,48},{1,17},{17,33},{33,49},{2,18},{18,34},{34,5... | collective-permute-start | bytes 110600 | tf_op jit(solution)/shard_map/ppermute | solution.py:21
  165.2 1.9 collective-permute-start.17
  167.6 5.0 %collective-permute-start.16 = (f32[4,18,18,1]{2,0,3,1:T(4,128)S(1)}, f32[4,18,18,1]{2,0,3,1:T(4,128)}, u32[]{:S(2)}, u32[]{:S(2)}) collective-permute-start(f32[4,18,18,1]{2,0,3,1:T(4,128)S(1)} %copy.63), channel_id=1, source_target_pairs={{0,1},{1,2},{2,3},{3,4},{4,5},{5,6},{6,7},{7,8},{8,9},{9,10},{10,1... | collective-permute-start | bytes 15560 | tf_op jit(solution)/shard_map/ppermute | solution.py:21
  175.1 1.3 copy.65
  179.3 1.4 collective-permute-start.19
  180.7 4.6 %collective-permute-start.18 = (f32[4,1,16,128]{3,2,1,0:T(8,128)S(1)}, f32[4,1,16,128]{3,2,1,0:T(8,128)S(1)}, u32[]{:S(2)}, u32[]{:S(2)}) collective-permute-start(f32[4,1,16,128]{3,2,1,0:T(8,128)S(1)} %get-tuple-element.30), channel_id=1, source_target_pairs={{0,64},{64,128},{128,192},{1,65},{65,129},{129,193},{2,66},{66,130... | collective-permute-start | bytes 98312 | tf_op jit(solution)/shard_map/ppermute | solution.py:21
  186.4 1.3 collective-permute-start.21
  187.7 4.6 %collective-permute-start.20 = (f32[4,18,1,128]{3,2,1,0:T(1,128)S(1)}, f32[4,18,1,128]{3,2,1,0:T(1,128)S(1)}, u32[]{:S(2)}, u32[]{:S(2)}) collective-permute-start(f32[4,18,1,128]{3,2,1,0:T(1,128)S(1)} %get-tuple-element.44), channel_id=1, source_target_pairs={{0,16},{16,32},{32,48},{1,17},{17,33},{33,49},{2,18},{18,34},{34,5... | collective-permute-start | bytes 110600 | tf_op jit(solution)/shard_map/ppermute | solution.py:21
  193.4 1.5 fusion.46
  195.0 1.7 copy.68
  196.7 1.9 collective-permute-start.23
  198.6 1.7 copy.67
  200.3 4.6 %collective-permute-start.22 = (f32[4,18,18,1]{2,0,3,1:T(4,128)S(1)}, f32[4,18,18,1]{2,0,3,1:T(4,128)S(1)}, u32[]{:S(2)}, u32[]{:S(2)}) collective-permute-start(f32[4,18,18,1]{2,0,3,1:T(4,128)S(1)} %copy.67), channel_id=1, source_target_pairs={{0,1},{1,2},{2,3},{3,4},{4,5},{5,6},{6,7},{7,8},{8,9},{9,10},{10,1... | collective-permute-start | bytes 15560 | tf_op jit(solution)/shard_map/ppermute | solution.py:21
  207.9 1.4 copy.72
  209.5 20.4 %gather_fusion = f32[2048]{0:T(1024)} fusion(f32[42120]{0:T(1024)S(1)} %reshape.467, s32[2048]{0:T(1024)S(1)} %fusion.41), kind=kCustom, calls=%fused_computation | custom fusion | bytes 24576 | tf_op jit(solution)/shard_map/gather | solution.py:153
  230.0 21.9 %all-to-all-start = ((f32[16,1,128]{2,1,0:T(1,128)}), f32[16,1,128]{2,1,0:T(1,128)}, u32[]{:S(2)}, u32[]{:S(2)}) async-start(f32[16,1,128]{2,1,0:T(1,128)} %bitcast.41), calls=%async_computation | async-start | bytes 16384 | tf_op jit(solution)/shard_map/all_to_all | solution.py:154
  252.1 20.6 %gather_fusion.1 = f32[2048]{0:T(1024)} fusion(f32[42120]{0:T(1024)S(1)} %reshape.469, s32[2048]{0:T(1024)S(1)} %fusion.41), kind=kCustom, calls=%fused_computation.1 | custom fusion | bytes 24576 | tf_op jit(solution)/shard_map/gather | solution.py:153
  272.9 20.4 %gather_fusion.2 = f32[2048]{0:T(1024)} fusion(f32[42120]{0:T(1024)S(1)} %reshape.470, s32[2048]{0:T(1024)S(1)} %fusion.41), kind=kCustom, calls=%fused_computation.2 | custom fusion | bytes 24576 | tf_op jit(solution)/shard_map/gather | solution.py:153
  293.9 1.5 copy.69
  295.4 2.2 pad_maximum_fusion.3
  299.5 9.6 %all-to-all-start.1 = ((f32[16,1,128]{2,1,0:T(1,128)}), f32[16,1,128]{2,1,0:T(1,128)}, u32[]{:S(2)}, u32[]{:S(2)}) async-start(f32[16,1,128]{2,1,0:T(1,128)} %bitcast.43), calls=%async_computation.1 | async-start | bytes 16384 | tf_op jit(solution)/shard_map/all_to_all | solution.py:154
  309.1 1.4 multiply_multiply_fusion.3
  311.3 7.2 %all-to-all-done.1 = f32[16,1,128]{2,1,0:T(1,128)} async-done(((f32[16,1,128]{2,1,0:T(1,128)}), f32[16,1,128]{2,1,0:T(1,128)}, u32[]{:S(2)}, u32[]{:S(2)}) %all-to-all-start.1) | async-done | bytes 8224 | tf_op jit(solution)/shard_map/all_to_all | solution.py:154
  318.5 4.7 %all-to-all-start.2 = ((f32[16,1,128]{2,1,0:T(1,128)}), f32[16,1,128]{2,1,0:T(1,128)}, u32[]{:S(2)}, u32[]{:S(2)}) async-start(f32[16,1,128]{2,1,0:T(1,128)} %bitcast.235), calls=%async_computation.2 | async-start | bytes 16384 | tf_op jit(solution)/shard_map/all_to_all | solution.py:154
  323.1 1.4 fusion.7
  324.8 20.7 %gather_fusion.3 = f32[2048]{0:T(1024)} fusion(f32[42120]{0:T(1024)S(1)} %reshape.471, s32[2048]{0:T(1024)} %copy-done.9), kind=kCustom, calls=%fused_computation.3 | custom fusion | bytes 24576 | tf_op jit(solution)/shard_map/gather | solution.py:153
  345.4 9.8 %all-to-all-start.3 = ((f32[16,1,128]{2,1,0:T(1,128)}), f32[16,1,128]{2,1,0:T(1,128)S(1)}, u32[]{:S(2)}, u32[]{:S(2)}) async-start(f32[16,1,128]{2,1,0:T(1,128)} %bitcast.47), calls=%async_computation.3 | async-start | bytes 16384 | tf_op jit(solution)/shard_map/all_to_all | solution.py:154
  356.3 8.3 %all-to-all-done.3 = f32[16,1,128]{2,1,0:T(1,128)S(1)} async-done(((f32[16,1,128]{2,1,0:T(1,128)}), f32[16,1,128]{2,1,0:T(1,128)S(1)}, u32[]{:S(2)}, u32[]{:S(2)}) %all-to-all-start.3) | async-done | bytes 8224 | tf_op jit(solution)/shard_map/all_to_all | solution.py:154
  (155 shorter events, 42.3 us)
Async XLA Ops:
  1.4 97.6 %collective-permute-start = (f32[4,1,16,128]{3,2,1,0:T(8,128)S(1)}, f32[4,1,16,128]{3,2,1,0:T(8,128)S(1)}, u32[]{:S(2)}, u32[]{:S(2)}) collective-permute-start(f32[4,1,16,128]{3,2,1,0:T(8,128)S(1)} %get-tuple-element.53), channel_id=1, source_target_pairs={{0,64},{64,128},{128,192},{1,65},{65,129},{129,193},{2,66},{66,130... | collective-permute-start | bytes 98312 | tf_op jit(solution)/shard_map/ppermute | solution.py:21
  5.4 93.7 %collective-permute-start.1 = (f32[4,1,16,128]{3,2,1,0:T(8,128)S(1)}, f32[4,1,16,128]{3,2,1,0:T(8,128)S(1)}, u32[]{:S(2)}, u32[]{:S(2)}) collective-permute-start(f32[4,1,16,128]{3,2,1,0:T(8,128)S(1)} %get-tuple-element.52), channel_id=1, source_target_pairs={{64,0},{128,64},{192,128},{65,1},{129,65},{193,129},{66,2},{130,66... | collective-permute-start | bytes 98312 | tf_op jit(solution)/shard_map/ppermute | solution.py:24
  49.2 49.8 %copy-start.2 = (f32[4,16,16,128]{3,2,1,0:T(8,128)S(1)}, f32[4,16,16,128]{3,2,1,0:T(8,128)}, u32[]{:S(2)}) copy-start(f32[4,16,16,128]{3,2,1,0:T(8,128)} %param.11) | copy-start | bytes 1572868
  99.1 5.4 %collective-permute-start.3 = (f32[4,18,1,128]{3,2,1,0:T(1,128)S(1)}, f32[4,18,1,128]{3,2,1,0:T(1,128)S(1)}, u32[]{:S(2)}, u32[]{:S(2)}) collective-permute-start(f32[4,18,1,128]{3,2,1,0:T(1,128)S(1)} %get-tuple-element.51), channel_id=1, source_target_pairs={{16,0},{32,16},{48,32},{17,1},{33,17},{49,33},{18,2},{34,18},{50,3... | collective-permute-start | bytes 110600 | tf_op jit(solution)/shard_map/ppermute | solution.py:24
  100.4 5.0 %collective-permute-start.2 = (f32[4,18,1,128]{3,2,1,0:T(1,128)S(1)}, f32[4,18,1,128]{3,2,1,0:T(1,128)S(1)}, u32[]{:S(2)}, u32[]{:S(2)}) collective-permute-start(f32[4,18,1,128]{3,2,1,0:T(1,128)S(1)} %get-tuple-element.50), channel_id=1, source_target_pairs={{0,16},{16,32},{32,48},{1,17},{17,33},{33,49},{2,18},{18,34},{34,5... | collective-permute-start | bytes 110600 | tf_op jit(solution)/shard_map/ppermute | solution.py:21
  106.5 7.9 %collective-permute-start.5 = (f32[4,18,18,1]{2,0,3,1:T(4,128)S(1)}, f32[4,18,18,1]{2,0,3,1:T(4,128)S(1)}, u32[]{:S(2)}, u32[]{:S(2)}) collective-permute-start(f32[4,18,18,1]{2,0,3,1:T(4,128)S(1)} %copy.55), channel_id=1, source_target_pairs={{1,0},{2,1},{3,2},{4,3},{5,4},{6,5},{7,6},{8,7},{9,8},{10,9},{11,1... | collective-permute-start | bytes 15560 | tf_op jit(solution)/shard_map/ppermute | solution.py:24
  111.0 4.1 %collective-permute-start.4 = (f32[4,18,18,1]{2,0,3,1:T(4,128)S(1)}, f32[4,18,18,1]{2,0,3,1:T(4,128)}, u32[]{:S(2)}, u32[]{:S(2)}) collective-permute-start(f32[4,18,18,1]{2,0,3,1:T(4,128)S(1)} %copy.54), channel_id=1, source_target_pairs={{0,1},{1,2},{2,3},{3,4},{4,5},{5,6},{6,7},{7,8},{8,9},{9,10},{10,1... | collective-permute-start | bytes 15560 | tf_op jit(solution)/shard_map/ppermute | solution.py:21
  118.6 5.5 %collective-permute-start.7 = (f32[4,1,16,128]{3,2,1,0:T(8,128)S(1)}, f32[4,1,16,128]{3,2,1,0:T(8,128)S(1)}, u32[]{:S(2)}, u32[]{:S(2)}) collective-permute-start(f32[4,1,16,128]{3,2,1,0:T(8,128)S(1)} %get-tuple-element.35), channel_id=1, source_target_pairs={{64,0},{128,64},{192,128},{65,1},{129,65},{193,129},{66,2},{130,66... | collective-permute-start | bytes 98312 | tf_op jit(solution)/shard_map/ppermute | solution.py:24
  119.9 5.0 %collective-permute-start.6 = (f32[4,1,16,128]{3,2,1,0:T(8,128)S(1)}, f32[4,1,16,128]{3,2,1,0:T(8,128)S(1)}, u32[]{:S(2)}, u32[]{:S(2)}) collective-permute-start(f32[4,1,16,128]{3,2,1,0:T(8,128)S(1)} %get-tuple-element.34), channel_id=1, source_target_pairs={{0,64},{64,128},{128,192},{1,65},{65,129},{129,193},{2,66},{66,130... | collective-permute-start | bytes 98312 | tf_op jit(solution)/shard_map/ppermute | solution.py:21
  124.1 7.8 %copy-start.7 = (f32[4,1,16,128]{3,2,1,0:T(8,128)}, f32[4,1,16,128]{3,2,1,0:T(8,128)S(1)}, u32[]{:S(2)}) copy-start(f32[4,1,16,128]{3,2,1,0:T(8,128)S(1)} %collective-permute-done.7) | copy-start | bytes 98308
  124.9 7.0 %copy-start.8 = (f32[4,1,16,128]{3,2,1,0:T(8,128)}, f32[4,1,16,128]{3,2,1,0:T(8,128)S(1)}, u32[]{:S(2)}) copy-start(f32[4,1,16,128]{3,2,1,0:T(8,128)S(1)} %collective-permute-done.6) | copy-start | bytes 98308
  124.9 5.9 %collective-permute-start.9 = (f32[4,18,1,128]{3,2,1,0:T(1,128)S(1)}, f32[4,18,1,128]{3,2,1,0:T(1,128)S(1)}, u32[]{:S(2)}, u32[]{:S(2)}) collective-permute-start(f32[4,18,1,128]{3,2,1,0:T(1,128)S(1)} %get-tuple-element.49), channel_id=1, source_target_pairs={{16,0},{32,16},{48,32},{17,1},{33,17},{49,33},{18,2},{34,18},{50,3... | collective-permute-start | bytes 110600 | tf_op jit(solution)/shard_map/ppermute | solution.py:24
  126.2 5.6 %collective-permute-start.8 = (f32[4,18,1,128]{3,2,1,0:T(1,128)S(1)}, f32[4,18,1,128]{3,2,1,0:T(1,128)S(1)}, u32[]{:S(2)}, u32[]{:S(2)}) collective-permute-start(f32[4,18,1,128]{3,2,1,0:T(1,128)S(1)} %get-tuple-element.48), channel_id=1, source_target_pairs={{0,16},{16,32},{32,48},{1,17},{17,33},{33,49},{2,18},{18,34},{34,5... | collective-permute-start | bytes 110600 | tf_op jit(solution)/shard_map/ppermute | solution.py:21
  130.8 1.0 copy-start.14
  134.0 10.2 %collective-permute-start.11 = (f32[4,18,18,1]{2,0,3,1:T(4,128)}, f32[4,18,18,1]{2,0,3,1:T(4,128)S(1)}, u32[]{:S(2)}, u32[]{:S(2)}) collective-permute-start(f32[4,18,18,1]{2,0,3,1:T(4,128)} %copy.60), channel_id=1, source_target_pairs={{1,0},{2,1},{3,2},{4,3},{5,4},{6,5},{7,6},{8,7},{9,8},{10,9},{11,1... | collective-permute-start | bytes 15560 | tf_op jit(solution)/shard_map/ppermute | solution.py:24
  138.2 6.6 %collective-permute-start.10 = (f32[4,18,18,1]{2,0,3,1:T(4,128)S(1)}, f32[4,18,18,1]{2,0,3,1:T(4,128)}, u32[]{:S(2)}, u32[]{:S(2)}) collective-permute-start(f32[4,18,18,1]{2,0,3,1:T(4,128)S(1)} %copy.59), channel_id=1, source_target_pairs={{0,1},{1,2},{2,3},{3,4},{4,5},{5,6},{6,7},{7,8},{8,9},{9,10},{10,1... | collective-permute-start | bytes 15560 | tf_op jit(solution)/shard_map/ppermute | solution.py:21
  149.1 6.1 %collective-permute-start.13 = (f32[4,1,16,128]{3,2,1,0:T(8,128)S(1)}, f32[4,1,16,128]{3,2,1,0:T(8,128)S(1)}, u32[]{:S(2)}, u32[]{:S(2)}) collective-permute-start(f32[4,1,16,128]{3,2,1,0:T(8,128)S(1)} %get-tuple-element.33), channel_id=1, source_target_pairs={{64,0},{128,64},{192,128},{65,1},{129,65},{193,129},{66,2},{130,66... | collective-permute-start | bytes 98312 | tf_op jit(solution)/shard_map/ppermute | solution.py:24
  150.4 5.6 %collective-permute-start.12 = (f32[4,1,16,128]{3,2,1,0:T(8,128)S(1)}, f32[4,1,16,128]{3,2,1,0:T(8,128)S(1)}, u32[]{:S(2)}, u32[]{:S(2)}) collective-permute-start(f32[4,1,16,128]{3,2,1,0:T(8,128)S(1)} %get-tuple-element.32), channel_id=1, source_target_pairs={{0,64},{64,128},{128,192},{1,65},{65,129},{129,193},{2,66},{66,130... | collective-permute-start | bytes 98312 | tf_op jit(solution)/shard_map/ppermute | solution.py:21
  155.2 7.8 %copy-start.3 = (f32[4,1,16,128]{3,2,1,0:T(8,128)}, f32[4,1,16,128]{3,2,1,0:T(8,128)S(1)}, u32[]{:S(2)}) copy-start(f32[4,1,16,128]{3,2,1,0:T(8,128)S(1)} %collective-permute-done.13) | copy-start | bytes 98308
  156.0 7.0 %copy-start.5 = (f32[4,1,16,128]{3,2,1,0:T(8,128)}, f32[4,1,16,128]{3,2,1,0:T(8,128)S(1)}, u32[]{:S(2)}) copy-start(f32[4,1,16,128]{3,2,1,0:T(8,128)S(1)} %collective-permute-done.12) | copy-start | bytes 98308
  156.1 5.9 %collective-permute-start.15 = (f32[4,18,1,128]{3,2,1,0:T(1,128)S(1)}, f32[4,18,1,128]{3,2,1,0:T(1,128)S(1)}, u32[]{:S(2)}, u32[]{:S(2)}) collective-permute-start(f32[4,18,1,128]{3,2,1,0:T(1,128)S(1)} %get-tuple-element.47), channel_id=1, source_target_pairs={{16,0},{32,16},{48,32},{17,1},{33,17},{49,33},{18,2},{34,18},{50,3... | collective-permute-start | bytes 110600 | tf_op jit(solution)/shard_map/ppermute | solution.py:24
  157.4 5.6 %collective-permute-start.14 = (f32[4,18,1,128]{3,2,1,0:T(1,128)S(1)}, f32[4,18,1,128]{3,2,1,0:T(1,128)S(1)}, u32[]{:S(2)}, u32[]{:S(2)}) collective-permute-start(f32[4,18,1,128]{3,2,1,0:T(1,128)S(1)} %get-tuple-element.46), channel_id=1, source_target_pairs={{0,16},{16,32},{32,48},{1,17},{17,33},{33,49},{2,18},{18,34},{34,5... | collective-permute-start | bytes 110600 | tf_op jit(solution)/shard_map/ppermute | solution.py:21
  162.0 1.0 copy-start.10
  164.0 8.7 %copy-start.20 = (f32[48]{0:T(128)S(1)}, f32[48]{0:T(128)}, u32[]{:S(2)}) copy-start(f32[48]{0:T(128)} %param.12) | copy-start | bytes 580
  165.2 9.4 %collective-permute-start.17 = (f32[4,18,18,1]{2,0,3,1:T(4,128)}, f32[4,18,18,1]{2,0,3,1:T(4,128)S(1)}, u32[]{:S(2)}, u32[]{:S(2)}) collective-permute-start(f32[4,18,18,1]{2,0,3,1:T(4,128)} %copy.64), channel_id=1, source_target_pairs={{1,0},{2,1},{3,2},{4,3},{5,4},{6,5},{7,6},{8,7},{9,8},{10,9},{11,1... | collective-permute-start | bytes 15560 | tf_op jit(solution)/shard_map/ppermute | solution.py:24
  167.6 7.5 %collective-permute-start.16 = (f32[4,18,18,1]{2,0,3,1:T(4,128)S(1)}, f32[4,18,18,1]{2,0,3,1:T(4,128)}, u32[]{:S(2)}, u32[]{:S(2)}) collective-permute-start(f32[4,18,18,1]{2,0,3,1:T(4,128)S(1)} %copy.63), channel_id=1, source_target_pairs={{0,1},{1,2},{2,3},{3,4},{4,5},{5,6},{6,7},{7,8},{8,9},{9,10},{10,1... | collective-permute-start | bytes 15560 | tf_op jit(solution)/shard_map/ppermute | solution.py:21
  174.5 1.9 copy-start.4
  174.5 1.9 copy-start.6
  174.5 1.9 copy-start.11
  174.5 1.9 copy-start.13
  177.9 1.0 copy-start.1
  179.3 13.0 %copy-start.19 = (s32[1,1,1,16,128]{4,3,2,1,0:T(8,128)S(1)}, s32[1,1,1,16,128]{4,3,2,1,0:T(8,128)}, u32[]{:S(2)}) copy-start(s32[1,1,1,16,128]{4,3,2,1,0:T(8,128)} %param.19) | copy-start | bytes 24580
  179.3 6.2 %collective-permute-start.19 = (f32[4,1,16,128]{3,2,1,0:T(8,128)S(1)}, f32[4,1,16,128]{3,2,1,0:T(8,128)S(1)}, u32[]{:S(2)}, u32[]{:S(2)}) collective-permute-start(f32[4,1,16,128]{3,2,1,0:T(8,128)S(1)} %get-tuple-element.31), channel_id=1, source_target_pairs={{64,0},{128,64},{192,128},{65,1},{129,65},{193,129},{66,2},{130,66... | collective-permute-start | bytes 98312 | tf_op jit(solution)/shard_map/ppermute | solution.py:24
  180.7 5.6 %collective-permute-start.18 = (f32[4,1,16,128]{3,2,1,0:T(8,128)S(1)}, f32[4,1,16,128]{3,2,1,0:T(8,128)S(1)}, u32[]{:S(2)}, u32[]{:S(2)}) collective-permute-start(f32[4,1,16,128]{3,2,1,0:T(8,128)S(1)} %get-tuple-element.30), channel_id=1, source_target_pairs={{0,64},{64,128},{128,192},{1,65},{65,129},{129,193},{2,66},{66,130... | collective-permute-start | bytes 98312 | tf_op jit(solution)/shard_map/ppermute | solution.py:21
  186.4 5.9 %collective-permute-start.21 = (f32[4,18,1,128]{3,2,1,0:T(1,128)S(1)}, f32[4,18,1,128]{3,2,1,0:T(1,128)S(1)}, u32[]{:S(2)}, u32[]{:S(2)}) collective-permute-start(f32[4,18,1,128]{3,2,1,0:T(1,128)S(1)} %get-tuple-element.45), channel_id=1, source_target_pairs={{16,0},{32,16},{48,32},{17,1},{33,17},{49,33},{18,2},{34,18},{50,3... | collective-permute-start | bytes 110600 | tf_op jit(solution)/shard_map/ppermute | solution.py:24
  187.7 5.6 %collective-permute-start.20 = (f32[4,18,1,128]{3,2,1,0:T(1,128)S(1)}, f32[4,18,1,128]{3,2,1,0:T(1,128)S(1)}, u32[]{:S(2)}, u32[]{:S(2)}) collective-permute-start(f32[4,18,1,128]{3,2,1,0:T(1,128)S(1)} %get-tuple-element.44), channel_id=1, source_target_pairs={{0,16},{16,32},{32,48},{1,17},{17,33},{33,49},{2,18},{18,34},{34,5... | collective-permute-start | bytes 110600 | tf_op jit(solution)/shard_map/ppermute | solution.py:21
  192.3 80.6 %copy-start.9 = (s32[2048]{0:T(1024)}, s32[2048]{0:T(1024)S(1)}, u32[]{:S(2)}) copy-start(s32[2048]{0:T(1024)S(1)} %fusion.41) | copy-start | bytes 24580
  195.0 10.0 %copy-start.21 = (s32[1,1,16,1]{2,3,1,0:T(1,128)S(1)}, s32[1,1,16,1]{2,3,1,0:T(1,128)}, u32[]{:S(2)}) copy-start(s32[1,1,16,1]{2,3,1,0:T(1,128)} %param.20) | copy-start | bytes 196
  196.7 96.6 %collective-permute-start.23 = (f32[4,18,18,1]{2,0,3,1:T(4,128)S(1)}, f32[4,18,18,1]{2,0,3,1:T(4,128)S(1)}, u32[]{:S(2)}, u32[]{:S(2)}) collective-permute-start(f32[4,18,18,1]{2,0,3,1:T(4,128)S(1)} %copy.68), channel_id=1, source_target_pairs={{1,0},{2,1},{3,2},{4,3},{5,4},{6,5},{7,6},{8,7},{9,8},{10,9},{11,1... | collective-permute-start | bytes 15560 | tf_op jit(solution)/shard_map/ppermute | solution.py:24
  200.3 93.6 %collective-permute-start.22 = (f32[4,18,18,1]{2,0,3,1:T(4,128)S(1)}, f32[4,18,18,1]{2,0,3,1:T(4,128)S(1)}, u32[]{:S(2)}, u32[]{:S(2)}) collective-permute-start(f32[4,18,18,1]{2,0,3,1:T(4,128)S(1)} %copy.67), channel_id=1, source_target_pairs={{0,1},{1,2},{2,3},{3,4},{4,5},{5,6},{6,7},{7,8},{8,9},{9,10},{10,1... | collective-permute-start | bytes 15560 | tf_op jit(solution)/shard_map/ppermute | solution.py:21
  230.0 69.5 %all-to-all-start = ((f32[16,1,128]{2,1,0:T(1,128)}), f32[16,1,128]{2,1,0:T(1,128)}, u32[]{:S(2)}, u32[]{:S(2)}) async-start(f32[16,1,128]{2,1,0:T(1,128)} %bitcast.41), calls=%async_computation | async-start | bytes 16384 | tf_op jit(solution)/shard_map/all_to_all | solution.py:154
  299.5 19.0 %all-to-all-start.1 = ((f32[16,1,128]{2,1,0:T(1,128)}), f32[16,1,128]{2,1,0:T(1,128)}, u32[]{:S(2)}, u32[]{:S(2)}) async-start(f32[16,1,128]{2,1,0:T(1,128)} %bitcast.43), calls=%async_computation.1 | async-start | bytes 16384 | tf_op jit(solution)/shard_map/all_to_all | solution.py:154
  318.5 27.0 %all-to-all-start.2 = ((f32[16,1,128]{2,1,0:T(1,128)}), f32[16,1,128]{2,1,0:T(1,128)}, u32[]{:S(2)}, u32[]{:S(2)}) async-start(f32[16,1,128]{2,1,0:T(1,128)} %bitcast.235), calls=%async_computation.2 | async-start | bytes 16384 | tf_op jit(solution)/shard_map/all_to_all | solution.py:154
  345.4 19.2 %copy-start = (f32[16,8,16,128]{3,1,2,0:T(8,128)S(1)}, f32[16,8,16,128]{3,1,2,0:T(8,128)}, u32[]{:S(2)}) copy-start(f32[16,8,16,128]{3,1,2,0:T(8,128)} %copy.72) | copy-start | bytes 3145732
  345.4 19.1 %all-to-all-start.3 = ((f32[16,1,128]{2,1,0:T(1,128)}), f32[16,1,128]{2,1,0:T(1,128)S(1)}, u32[]{:S(2)}, u32[]{:S(2)}) async-start(f32[16,1,128]{2,1,0:T(1,128)} %bitcast.47), calls=%async_computation.3 | async-start | bytes 16384 | tf_op jit(solution)/shard_map/all_to_all | solution.py:154
  355.3 10.3 %copy-start.18 = (f32[2048]{0:T(1024)S(1)}, f32[2048]{0:T(1024)}, u32[]{:S(2)}) copy-start(f32[2048]{0:T(1024)} %select_bitcast_fusion) | copy-start | bytes 24580
  356.3 9.3 %copy-start.16 = (f32[128,48]{0,1:T(8,128)S(1)}, f32[128,48]{0,1:T(8,128)}, u32[]{:S(2)}) copy-start(f32[128,48]{0,1:T(8,128)} %get-tuple-element.54) | copy-start | bytes 73732
  356.3 9.3 %copy-start.17 = (f32[128,48]{0,1:T(8,128)S(1)}, f32[128,48]{0,1:T(8,128)}, u32[]{:S(2)}) copy-start(f32[128,48]{0,1:T(8,128)} %get-tuple-element.55) | copy-start | bytes 73732
  (2 other events, 1.2 us)
where the time goes:
time: 371 us; the launch traced here: 367 us
  local copies, waits for them, and re-layouts  166 us (45%)
  starting transfers between devices  120 us (32%)
  other arithmetic  54.7 us (15%)
  waiting for transfers between devices  21.9 us (6%)
    gather x4, local copies, waits for them, and re-layouts, body(): sampled = pressure.reshape(-1)[sample_flat]  82.1 us
    ppermute x12, starting transfers between devices, padded(): lax.ppermute(lax.slice_in_dim(block, block.shape[dim] - width, None, axis...  52.3 us
    slice x1, local copies, waits for them, and re-layouts, body(): pressure = pressure + source_map[:, opening].reshape(wide_x, wide_y, wide_z)  49.8 us
    all_to_all x4, starting transfers between devices, body(): lax.all_to_all(sampled, 'gz', split_axis=0, concat_axis=0, tiled=True)  46 us
    scatter-add x1, other arithmetic, body(): source_map = jnp.zeros((wide_x * wide_y * wide_z, STEPS), jnp.float32).at...  37.4 us
    ppermute x12, starting transfers between devices, padded(): lax.ppermute(lax.slice_in_dim(block, 0, width, axis=dim), axis, backward)  21.9 us
    all_to_all x4, waiting for transfers between devices, body(): lax.all_to_all(sampled, 'gz', split_axis=0, concat_axis=0, tiled=True)  15.5 us
  transfers between devices with their start and end apart: 28, of which 10 were waited for; matrix products, arithmetic and copies ran while one was open for 54% of the time, Pallas kernels for 0%

commit v1 on v0

v1 whole, which is shorter than its diff:
```python
import jax
import jax.numpy as jnp
from jax import lax
from jax.experimental import pallas as pl
from jax.experimental.pallas import tpu as pltpu
from jax.sharding import PartitionSpec as P

STEPS = 4
HIST = 124
SOURCES = 48
TONES = 48
MODES = 2000
SRC = 4096
TX, TY, TZ = 16, 16, 128
ROWS = TX * TY
OWN = 16
CAP = 128
SLOTS = OWN * CAP
NB = 2 * TONES
KC = 1024
F32 = jnp.float32
BF = jnp.bfloat16
MESH = pl.DeviceIdType.MESH


def split(values):
    high = values.astype(BF)
    return high, (values - high.astype(F32)).astype(BF)


def dot_nn(a, b):
    return lax.dot_general(a, b, (((1,), (0,)), ((), ())), preferred_element_type=F32)


def dot_nt(a, b):
    return lax.dot_general(a, b, (((1,), (1,)), ((), ())), preferred_element_type=F32)


def half_wave(x, half):
    k = jnp.floor(x * 0.3183098861837907 + (0.5 - half))
    h = k + half
    r = x - h * 3.140625
    r = r - h * 0.0009670257568359375
    r = r - h * 6.2771141529083251953e-07
    q = r * r
    s = -2.505210838544172e-08
    for c in (2.7557319223985893e-06, -1.984126984126984e-04, 8.333333333333333e-03, -0.16666666666666666):
        s = s * q + c
    s = r + r * q * s
    sign = 1.0 - 2.0 * (k - 2.0 * jnp.floor(k * 0.5))
    return jnp.where(half > 0.25, -sign, sign) * s


def iota(shape, dim):
    return lax.broadcasted_iota(jnp.int32, shape, dim)


def kernel(
    fields_h, tone_r, mfreq_r, mamp_r, mmap_r, spos_r, sid_r, sgain_r, cell_r, count_r, hist_h,
    fout_h, cout_h,
    fv, hv, pst, uv, psum, ms, wv, srow, scol, acc, cone, rsel, ov, bt, sb, rb,
    ys, zs, gxm, gxp, gym, gyp, gzm, gzp, gvx, gvy, svy,
    fsem, hsem, osem, ss, rs, vss, vrs, ass, ars,
):
    ix = lax.axis_index("gx")
    iy = lax.axis_index("gy")
    iz = lax.axis_index("gz")
    low_x, high_x = ix == 0, ix == 3
    low_y, high_y = iy == 0, iy == 3
    low_z, high_z = iz == 0, iz == OWN - 1

    loads = [pltpu.make_async_copy(fields_h.at[k], fv.at[k], fsem.at[k]) for k in range(4)]
    for k in (0, 3, 1, 2):
        loads[k].start()
    hist_load = pltpu.make_async_copy(hist_h, hv.at[pl.ds(0, HIST * OWN)], hsem)
    hist_load.start()

    barrier = pltpu.get_barrier_semaphore()
    for k in range(1, OWN):
        pl.semaphore_signal(barrier, inc=1, device_id={"gz": lax.rem(iz + k, OWN)}, device_id_type=MESH)

    sides = (
        (jnp.logical_not(low_x), {"gx": ix - 1}),
        (jnp.logical_not(high_x), {"gx": ix + 1}),
        (jnp.logical_not(low_y), {"gy": iy - 1}),
        (jnp.logical_not(high_y), {"gy": iy + 1}),
        (jnp.logical_not(low_z), {"gz": iz - 1}),
        (jnp.logical_not(high_z), {"gz": iz + 1}),
    )
    for has, target in sides[:4]:
        @pl.when(has)
        def _(target=target):
            pl.semaphore_signal(barrier, inc=1, device_id=target, device_id_type=MESH)

    row8 = iota((8, 1), 0)
    ms[...] = jnp.zeros_like(ms)
    ms[0:1, 0:MODES] = mfreq_r[...]
    ms[1:2, 0:MODES] = mamp_r[...]
    ms[2:3, 0:MODES] = mmap_r[...].astype(F32)
    moment = (HIST + row8 % STEPS).astype(F32)
    waves = ms[1:2, :] * half_wave(ms[0:1, :] * moment, jnp.zeros((8, 1), F32))
    high = waves.astype(BF).astype(F32)
    waves = jnp.where(row8 < STEPS, high, waves - high).astype(BF)
    pick = jnp.where(iota((SOURCES, 1), 0).astype(F32) == ms[2:3, :], 1.0, 0.0).astype(BF)
    drive = dot_nt(waves, pick)
    drive = drive + pltpu.roll(drive, 4, 0)
    high = drive.astype(BF).astype(F32)
    drive = jnp.where(row8 < STEPS, high, drive - high).astype(BF)
    pick = jnp.where(iota((SOURCES, 1), 0) == sid_r[...], 1.0, 0.0).astype(BF)
    weight = dot_nn(drive, pick)
    weight = (weight + pltpu.roll(weight, 4, 0)) * sgain_r[...]
    high = weight.astype(BF).astype(F32)
    wv[...] = jnp.where(row8 < STEPS, high, weight - high)
    lx = spos_r[0:1, :] - ix * TX
    ly = spos_r[1:2, :] - iy * TY
    lz = spos_r[2:3, :] - iz * TZ
    inside = (lx >= 0) & (lx < TX) & (ly >= 0) & (ly < TY) & (lz >= 0) & (lz < TZ)
    srow[...] = jnp.where(inside, lx * TY + ly, -1).astype(F32)
    scol[...] = lz.astype(F32)

    lane = iota((1, TZ), 1)
    even = lane % 2 == 0

    def z_pack(slabs, base, packed):
        for i, piece in slabs:
            turned = pltpu.roll(piece, (base + 2 * i) % TZ, 1) if (base + 2 * i) % TZ else piece
            here = ((lane + 1 - base + TZ) % TZ) // 2 == i
            packed = jnp.where(here, turned, packed)
        return packed

    def pieces(ref, n):
        return [(i, ref[n, i * 8:(i + 1) * 8, :]) for i in range(ROWS // 8)]

    def face_copies(n):
        src = pst.at[n]
        ends = (
            (src.at[pl.ds(0, TY)], gxp.at[n]),
            (src.at[pl.ds(ROWS - TY, TY)], gxm.at[n]),
            (ys.at[n, 0], gyp.at[n]),
            (ys.at[n, 1], gym.at[n]),
            (zs.at[n], gzp.at[n]),
            (zs.at[n], gzm.at[n]),
        )
        return [
            (has, pltpu.make_async_remote_copy(
                src_ref=a, dst_ref=b, send_sem=ss.at[n, i], recv_sem=rs.at[n, i],
                device_id=target, device_id_type=MESH))
            for i, ((has, target), (a, b)) in enumerate(zip(sides, ends))
        ]

    def send_faces(n):
        for has, copy in face_copies(n):
            @pl.when(has)
            def _(copy=copy):
                copy.start()

    def recv_faces(n):
        copies = face_copies(n)
        for i in range(6):
            has = sides[i ^ 1][0]
            copy = copies[i][1]
            @pl.when(has)
            def _(copy=copy):
                copy.wait_recv()

    def y_faces(n):
        ys[n, 0] = pst[n, pl.ds(0, TX, stride=TY), :]
        ys[n, 1] = pst[n, pl.ds(TY - 1, TX, stride=TY), :]

    for k in (0, 3, 1, 2):
        loads[k].wait()
    pst[0] = fv[0]
    y_faces(0)
    svy[...] = fv[2, pl.ds(TY - 1, TX, stride=TY), :]
    packed = z_pack(pieces(fv, 0), 0, jnp.zeros((8, TZ), F32))
    zs[0] = z_pack(pieces(fv, 3), 64, packed)

    expected = (
        OWN - 1
        + jnp.where(low_x, 0, 1) + jnp.where(high_x, 0, 1)
        + jnp.where(low_y, 0, 1) + jnp.where(high_y, 0, 1)
    )
    pl.semaphore_wait(barrier, expected)
    send_faces(0)
    vx_copy = pltpu.make_async_remote_copy(
        src_ref=fv.at[1, pl.ds(ROWS - TY, TY)], dst_ref=gvx, send_sem=vss.at[0], recv_sem=vrs.at[0],
        device_id=sides[1][1], device_id_type=MESH)
    vy_copy = pltpu.make_async_remote_copy(
        src_ref=svy, dst_ref=gvy, send_sem=vss.at[1], recv_sem=vrs.at[1],
        device_id=sides[3][1], device_id_type=MESH)

    @pl.when(sides[1][0])
    def _():
        vx_copy.start()

    @pl.when(sides[3][0])
    def _():
        vy_copy.start()

    acc[...] = jnp.zeros_like(acc)

    @pl.loop(0, SRC // KC)
    def _(chunk):
        span = pl.ds(pl.multiple_of(chunk * KC, KC), KC)
        a = jnp.where(iota((ROWS, 1), 0).astype(F32) == srow[:, span], 1.0, 0.0).astype(BF)
        m = iota((TZ, 1), 0).astype(F32) == scol[:, span]
        b = jnp.concatenate([jnp.where(m, wv[q:q + 1, span], 0.0).astype(BF) for q in range(2 * STEPS)], axis=0)
        acc[...] += dot_nt(a, b)

    eye = iota((TONES, TONES), 0) == iota((TONES, TONES), 1)
    freq = jnp.sum(jnp.where(eye, tone_r[...], 0.0), axis=1, keepdims=True)
    freq = jnp.concatenate([freq, freq], axis=0)
    angle = freq * lane.astype(F32)
    basis = half_wave(angle, jnp.where(iota((NB, 1), 0) < TONES, 0.5, 0.0).astype(F32)) * 0.125
    for n in range(STEPS):
        bt[n * NB:(n + 1) * NB, :] = jnp.broadcast_to(basis[:, HIST + n:HIST + n + 1], (NB, CAP))

    live = jnp.where(lane < count_r[...], 1.0, 0.0).astype(F32)
    hist_load.wait()
    hv[HIST * OWN:, :] = jnp.zeros((STEPS * OWN, CAP), F32)
    bh, bl = split(basis)
    lhs = jnp.concatenate([bh, bl, bh], axis=1)
    for e in range(0, OWN, 2):
        hh, hl = split(jnp.concatenate(
            [hv[pl.ds(e, HIST + STEPS, stride=OWN), :], hv[pl.ds(e + 1, HIST + STEPS, stride=OWN), :]], axis=1))
        part = dot_nn(lhs, jnp.concatenate([hh, hh, hl], axis=0))
        ov[pl.ds(e, NB, stride=OWN), :] = part[:, :CAP] * live[e:e + 1]
        ov[pl.ds(e + 1, NB, stride=OWN), :] = part[:, CAP:] * live[e + 1:e + 2]

    for d in range(OWN):
        cells = cell_r[d:d + 1, :]
        span = slice(d * CAP, (d + 1) * CAP)
        one = jnp.where(iota((TZ, 1), 0) == cells % TZ, 1.0, 0.0).astype(BF)
        cone[0:TZ, span] = one
        cone[TZ:2 * TZ, span] = one
        rsel[:, span] = cells // TZ
    sb[...] = jnp.zeros_like(sb)

    def listen(n):
        lhs = jnp.concatenate(split(pst[n + 1]), axis=1)
        for d in range(0, OWN, 2):
            span = slice(d * CAP, (d + 2) * CAP)
            seen = dot_nn(lhs, cone[:, span])
            got = jnp.sum(jnp.where(iota((ROWS, 1), 0) == rsel[:, span], seen, 0.0), axis=0, keepdims=True)
            sb[d * 8 + n:d * 8 + n + 1, :] = got[:, :CAP]
            sb[(d + 1) * 8 + n:(d + 1) * 8 + n + 1, :] = got[:, CAP:]

    sub = iota((TY, 1), 0)

    def behind(get, x, gx, gy, merged):
        own = get(x)
        xm = get(x - 1) if x else gx
        ym = jnp.where(sub == 0, gy[x:x + 1, :], pltpu.roll(own, 1, 0))
        ring = jnp.concatenate([roll_lanes(merged, -4 * x), roll_lanes(merged, -4 * x - 2)], axis=0)
        zm = pltpu.roll(jnp.where(lane == TZ - 1, ring, own), 1, 1)
        return xm, ym, zm

    def ahead(get, x, gx, gy, merged):
        own = get(x)
        xp = get(x + 1) if x < TX - 1 else gx
        yp = jnp.where(sub == TY - 1, gy[x:x + 1, :], pltpu.roll(own, TY - 1, 0))
        ring = jnp.concatenate([roll_lanes(merged, -4 * x), roll_lanes(merged, -4 * x - 2)], axis=0)
        zp = pltpu.roll(jnp.where(lane == 0, ring, own), TZ - 1, 1)
        return xp, yp, zp

    def roll_lanes(v, by):
        return pltpu.roll(v, by % TZ, 1) if by % TZ else v

    def slab(ref, x):
        return ref[x * TY:(x + 1) * TY, :]

    @pl.when(jnp.logical_not(low_x))
    def _():
        vx_copy.wait_recv()

    @pl.when(jnp.logical_not(low_y))
    def _():
        vy_copy.wait_recv()

    recv_faces(0)
    from_low = jnp.where(low_z, 0.0, gzm[0])
    vzg = roll_lanes(from_low, -64)
    vxg = jnp.where(low_x, 0.0, gvx[...])
    vyg = jnp.where(low_y, 0.0, gvy[...])
    for x in range(TX):
        own = [slab(fv.at[k], x) for k in (1, 2, 3)]
        xm = slab(fv.at[1], x - 1) if x else vxg
        ym = jnp.where(sub == 0, vyg[x:x + 1, :], pltpu.roll(own[1], 1, 0))
        ring = jnp.concatenate([roll_lanes(vzg, -4 * x), roll_lanes(vzg, -4 * x - 2)], axis=0)
        zm = pltpu.roll(jnp.where(lane == TZ - 1, ring, own[2]), 1, 1)
        uv[x * TY:(x + 1) * TY, :] = 0.5 * ((own[0] - xm) + (own[1] - ym) + (own[2] - zm))

    gx_sum = jnp.zeros((TY, TZ), F32)
    gy_sum = jnp.zeros((TX, TZ), F32)
    gz_sum = jnp.zeros((8, TZ), F32)
    for n in range(STEPS):
        if n:
            recv_faces(n)
        get = lambda x, n=n: pst[n, x * TY:(x + 1) * TY, :]
        xg = jnp.where(high_x, 0.0, gxp[n])
        yg = jnp.where(high_y, 0.0, gyp[n])
        zg = jnp.where(high_z, 0.0, gzp[n])
        gx_sum, gy_sum, gz_sum = gx_sum + xg, gy_sum + yg, gz_sum + zg
        xl = jnp.where(low_x, get(0), gxm[n])
        yl = jnp.where(low_y, ys[n, 0], gym[n])
        zl = jnp.where(low_z, roll_lanes(zs[n], -1), gzm[n])
        merged = jnp.where(even, zg, zl)
        for x in range(TX):
            at = slice(x * TY, (x + 1) * TY)
            own = get(x)
            xm, ym, zm = behind(get, x, xl, yl, merged)
            xp, yp, zp = ahead(get, x, xg, yg, merged)
            lap = (xm + xp) + (ym + yp) + (zm + zp) - 6.0 * own
            u = uv[at, :] - 0.25 * lap
            uv[at, :] = u
            new = own - u + (acc[at, n * TZ:(n + 1) * TZ] + acc[at, (STEPS + n) * TZ:(STEPS + n + 1) * TZ])
            pst[n + 1, at, :] = new
            psum[at, :] = own if n == 0 else psum[at, :] + own
        if n < STEPS - 1:
            y_faces(n + 1)
            zs[n + 1] = z_pack(pieces(pst, n + 1), 0, jnp.zeros((8, TZ), F32))
            send_faces(n + 1)
        listen(n)

    def block_copy(k):
        target = lax.rem(iz + k, OWN)
        return pltpu.make_async_remote_copy(
            src_ref=sb.at[pl.ds(pl.multiple_of(target * 8, 8), 8)],
            dst_ref=rb.at[pl.ds(pl.multiple_of(iz * 8, 8), 8)],
            send_sem=ass.at[k], recv_sem=ars.at[k], device_id={"gz": target}, device_id_type=MESH)

    sends = [block_copy(k) for k in range(1, OWN)]
    for copy in sends:
        copy.start()
    mine = pl.ds(pl.multiple_of(iz * 8, 8), 8)
    rb[mine, :] = sb[mine, :]

    for n in range(STEPS):
        for has, copy in face_copies(n):
            @pl.when(has)
            def _(copy=copy):
                copy.wait_send()

    @pl.when(sides[1][0])
    def _():
        vx_copy.wait_send()

    @pl.when(sides[3][0])
    def _():
        vy_copy.wait_send()

    outs = [pltpu.make_async_copy(pst.at[STEPS], fout_h.at[0], osem.at[0])]
    outs[0].start()
    total = lambda x: slab(psum, x)
    for x in range(TX):
        at = slice(x * TY, (x + 1) * TY)
        own = total(x)
        xp, yp, zp = ahead(total, x, gx_sum, gy_sum, gz_sum)
        fv[1, at, :] = fv[1, at, :] - 0.5 * (xp - own)
        fv[2, at, :] = fv[2, at, :] - 0.5 * (yp - own)
        fv[3, at, :] = fv[3, at, :] - 0.5 * (zp - own)
    outs.append(pltpu.make_async_copy(fv.at[pl.ds(1, 3)], fout_h.at[pl.ds(1, 3)], osem.at[1]))
    outs[1].start()

    for copy in sends:
        copy.wait_recv()
    heard = [rb[pl.ds(n, OWN, stride=8), :] * live for n in range(STEPS)]
    parts = 4
    per = NB // parts
    for part in range(parts):
        for j in range(part * per, (part + 1) * per):
            at = slice(j * OWN, (j + 1) * OWN)
            term = ov[at, :]
            for n in range(STEPS):
                term = term + bt[n * NB + j:n * NB + j + 1, :] * heard[n]
            ov[at, :] = term
        rows = pl.ds(part * per * OWN, per * OWN)
        outs.append(pltpu.make_async_copy(ov.at[rows], cout_h.at[rows], osem.at[2 + part]))
        outs[-1].start()
    for copy in sends:
        copy.wait_send()
    for copy in outs:
        copy.wait()


def body(
    fields, tone_freq, mode_freq, mode_amp, mode_map, src_pos, src_id, src_gain, sample_cell, sample_count, history
):
    vmem = pl.BlockSpec(memory_space=pltpu.VMEM)
    hbm = pl.BlockSpec(memory_space=pl.ANY)
    face = (STEPS, TY, TZ)
    fields_out, coefficients = pl.pallas_call(
        kernel,
        out_shape=(
            jax.ShapeDtypeStruct((4, ROWS, TZ), F32),
            jax.ShapeDtypeStruct((NB * OWN, CAP), F32),
        ),
        in_specs=[hbm] + [vmem] * 9 + [hbm],
        out_specs=(hbm, hbm),
        scratch_shapes=[
            pltpu.VMEM((4, ROWS, TZ), F32),
            pltpu.VMEM(((HIST + STEPS) * OWN, CAP), F32),
            pltpu.VMEM((STEPS + 1, ROWS, TZ), F32),
            pltpu.VMEM((ROWS, TZ), F32),
            pltpu.VMEM((ROWS, TZ), F32),
            pltpu.VMEM((8, 2048), F32),
            pltpu.VMEM((8, SRC), F32),
            pltpu.VMEM((1, SRC), F32),
            pltpu.VMEM((1, SRC), F32),
            pltpu.VMEM((ROWS, 2 * STEPS * TZ), F32),
            pltpu.VMEM((2 * TZ, SLOTS), BF),
            pltpu.VMEM((1, SLOTS), jnp.int32),
            pltpu.VMEM((NB * OWN, CAP), F32),
            pltpu.VMEM((STEPS * NB, CAP), F32),
            pltpu.VMEM((OWN * 8, CAP), F32),
            pltpu.VMEM((OWN * 8, CAP), F32),
            pltpu.VMEM((STEPS, 2, TX, TZ), F32),
            pltpu.VMEM((STEPS, 8, TZ), F32),
            pltpu.VMEM(face, F32),
            pltpu.VMEM(face, F32),
            pltpu.VMEM(face, F32),
            pltpu.VMEM(face, F32),
            pltpu.VMEM((STEPS, 8, TZ), F32),
            pltpu.VMEM((STEPS, 8, TZ), F32),
            pltpu.VMEM((TY, TZ), F32),
            pltpu.VMEM((TX, TZ), F32),
            pltpu.VMEM((TX, TZ), F32),
            pltpu.SemaphoreType.DMA((4,)),
            pltpu.SemaphoreType.DMA,
            pltpu.SemaphoreType.DMA((6,)),
            pltpu.SemaphoreType.DMA((STEPS, 6)),
            pltpu.SemaphoreType.DMA((STEPS, 6)),
            pltpu.SemaphoreType.DMA((2,)),
            pltpu.SemaphoreType.DMA((2,)),
            pltpu.SemaphoreType.DMA((OWN,)),
            pltpu.SemaphoreType.DMA((OWN,)),
        ],
        compiler_params=pltpu.CompilerParams(
            collective_id=0, has_side_effects=True, vmem_limit_bytes=40 * 1024 * 1024
        ),
    )(
        fields.reshape(4, ROWS, TZ),
        tone_freq.reshape(1, TONES),
        mode_freq.reshape(1, MODES),
        mode_amp.reshape(1, MODES),
        mode_map.reshape(1, MODES),
        src_pos,
        src_id.reshape(1, SRC),
        src_gain.reshape(1, SRC),
        sample_cell.reshape(OWN, CAP),
        sample_count.reshape(OWN, 1),
        history.reshape(HIST * OWN, CAP),
    )
    return fields_out.reshape(fields.shape), coefficients.reshape(NB, 1, 1, 1, OWN, CAP)


def solution(mesh):
    in_specs = (
        P(None, "gx", "gy", "gz"),
        P(),
        P(),
        P(),
        P(),
        P(),
        P(),
        P(),
        P("gx", "gy", "gz", None, None),
        P("gx", "gy", None, "gz"),
        P(None, "gx", "gy", "gz", None, None),
    )
    out_specs = (P(None, "gx", "gy", "gz"), P(None, "gx", "gy", "gz", None, None))
    return jax.shard_map(body, mesh=mesh, in_specs=in_specs, out_specs=out_specs, check_vma=False)
```

time: 371 us -> 50.4 us (0.14)
  local copies, waits for them, and re-layouts: 166 us -> 8.88 us
  starting transfers between devices: 120 us -> 0 us
  other arithmetic: 54.7 us -> 0 us
  Pallas kernels: 0 us -> 40.4 us
  waiting for transfers between devices: 21.9 us -> 0 us
    gather x4 -> x0, local copies, waits for them, and re-layouts: 82.1 us -> none  [body(): sampled = pressure.reshape(-1)[sample_flat]]
    ppermute x24 -> x0, starting transfers between devices: 74.2 us -> none  [the longest x12 52.3 us: padded(): lax.ppermute(lax.slice_in_dim(block, block.shape[dim] - width, None, axis...]
    slice x31 -> x0, local copies, waits for them, and re-layouts: 64.2 us -> none  [the longest x1 49.8 us: body(): pressure = pressure + source_map[:, opening].reshape(wide_x, wide_y, wide_z)]
    all_to_all x4 -> x0, starting transfers between devices: 46 us -> none  [body(): lax.all_to_all(sampled, 'gz', split_axis=0, concat_axis=0, tiled=True)]
    pallas_call x0 -> x1, Pallas kernels: none -> 40.4 us  [body(): pl.pallas_call(kernel, out_shape=(jax.ShapeDtypeStruct((4, ROWS, TZ), F32...]
    scatter-add x1 -> x0, other arithmetic: 37.4 us -> none  [body(): source_map = jnp.zeros((wide_x * wide_y * wide_z, STEPS), jnp.float32).at...]
    all_to_all x4 -> x0, waiting for transfers between devices: 15.5 us -> none  [body(): lax.all_to_all(sampled, 'gz', split_axis=0, concat_axis=0, tiled=True)]
    ppermute x8 -> x0, local copies, waits for them, and re-layouts: 7.75 us -> none  [the longest x4 5.5 us: padded(): lax.ppermute(lax.slice_in_dim(block, block.shape[dim] - width, None, axis...]
  transfers between devices with their start and end apart: 28 -> 0, of which waited for: 10 -> 0; matrix products, arithmetic and copies ran while one was open for 54% -> 0% of each run, Pallas kernels for 0% -> 0%
where the time goes in v1:
time: 50.4 us; the launch traced here: 49.9 us
  Pallas kernels  40.4 us (80%)
  local copies, waits for them, and re-layouts  8.88 us (18%)
  between operations  0.67 us (1%)
    pallas_call x1, Pallas kernels, body(): pl.pallas_call(kernel, out_shape=(jax.ShapeDtypeStruct((4, ROWS, TZ), F32...  40.4 us
    unnamed x24, local copies, waits for them, and re-layouts  8.79 us

profile of v1, /device:TPU:1, one launch (start us, length us, event | category | flops | bytes accessed | tf_op | source)
XLA Modules:
  0.0 49.9 jit_solution(9714288736884776049)
XLA Ops:
  0.6 0.0 copy-start.3
  0.6 0.0 copy-start.10
  0.7 0.0 copy-start.5
  0.7 0.6 %copy-done.10 = s32[1,1,16,1]{2,3,1,0:T(1,128)S(1)} copy-done((s32[1,1,16,1]{2,3,1,0:T(1,128)S(1)}, s32[1,1,16,1]{2,3,1,0:T(1,128)}, u32[]{:S(2)}) %copy-start.10) | copy-done | bytes 88
  1.3 0.0 copy-start.9
  1.3 0.1 copy.13.count_r
  1.4 0.0 copy-done.3
  1.4 0.0 copy-done.5
  1.4 0.6 %copy-done.9 = f32[48]{0:T(128)S(1)} copy-done((f32[48]{0:T(128)S(1)}, f32[48]{0:T(128)}, u32[]{:S(2)}) %copy-start.9) | copy-done | bytes 216
  2.0 0.0 copy-start
  2.0 1.2 %copy-done = f32[124,1,1,1,16,128]{5,4,3,2,1,0:T(8,128)S(1)} copy-done((f32[124,1,1,1,16,128]{5,4,3,2,1,0:T(8,128)S(1)}, f32[124,1,1,1,16,128]{5,4,3,2,1,0:T(8,128)}, u32[]{:S(2)}) %copy-start) | copy-done | bytes 1015832
  3.2 0.0 copy-start.1
  3.2 1.0 %copy-done.1 = f32[4,16,16,128]{3,2,1,0:T(8,128)S(1)} copy-done((f32[4,16,16,128]{3,2,1,0:T(8,128)S(1)}, f32[4,16,16,128]{3,2,1,0:T(8,128)}, u32[]{:S(2)}) %copy-start.1) | copy-done | bytes 524312
  4.2 0.0 copy-start.2
  4.2 0.8 %copy-done.2 = s32[3,4096]{1,0:T(4,128)S(1)} copy-done((s32[3,4096]{1,0:T(4,128)S(1)}, s32[3,4096]{1,0:T(4,128)}, u32[]{:S(2)}) %copy-start.2) | copy-done | bytes 49176
  5.1 0.0 copy-start.4
  5.1 0.7 %copy-done.4 = f32[4096]{0:T(1024)S(1)} copy-done((f32[4096]{0:T(1024)S(1)}, f32[4096]{0:T(1024)}, u32[]{:S(2)}) %copy-start.4) | copy-done | bytes 16408
  5.8 0.0 copy-start.6
  5.8 0.7 %copy-done.6 = f32[2000]{0:T(1024)S(1)} copy-done((f32[2000]{0:T(1024)S(1)}, f32[2000]{0:T(1024)}, u32[]{:S(2)}) %copy-start.6) | copy-done | bytes 8024
  6.5 0.0 copy-start.7
  6.5 0.7 %copy-done.7 = s32[2000]{0:T(1024)S(1)} copy-done((s32[2000]{0:T(1024)S(1)}, s32[2000]{0:T(1024)}, u32[]{:S(2)}) %copy-start.7) | copy-done | bytes 8024
  7.2 0.0 copy-start.8
  7.2 0.7 %copy-done.8 = s32[1,1,1,16,128]{4,3,2,1,0:T(8,128)S(1)} copy-done((s32[1,1,1,16,128]{4,3,2,1,0:T(8,128)S(1)}, s32[1,1,1,16,128]{4,3,2,1,0:T(8,128)}, u32[]{:S(2)}) %copy-start.8) | copy-done | bytes 8216
  7.9 40.4 %shard_map.122 = (f32[4,256,128]{2,1,0:T(8,128)S(1)}, f32[1536,128]{1,0:T(8,128)S(1)}) custom-call(f32[4,256,128]{2,1,0:T(8,128)S(1)} %bitcast.16, f32[1,48]{1,0:T(1,128)S(1)} %bitcast.24, f32[1,2000]{1,0:T(1,128)S(1)} %bitcast.20, f32[1,2000]{1,0:T(1,128)S(1)} %bitcast.21, s32[1,2000]{1,0:T(1,128)S(1)} %bitcast.22, s32[3,4096]{1,0:T(4,128)S(1)} %copy-done.2, ...), custom_call_target="tpu_custom_call" | custom-call | tf_op jit(solution)/shard_map/pallas_call | solution.py:392
  48.2 0.8 %copy.17 = f32[4,16,16,128]{3,2,1,0:T(8,128)} copy(f32[4,16,16,128]{3,2,1,0:T(8,128)S(1)} %bitcast.17) | data formatting | bytes 1048576
  49.0 0.9 %copy.18 = f32[96,1,1,1,16,128]{5,4,3,2,1,0:T(8,128)} copy(f32[96,1,1,1,16,128]{5,4,3,2,1,0:T(8,128)S(1)} %bitcast.15) | data formatting | bytes 1572864
Async XLA Ops:
  0.6 0.8 %copy-start.3 = (s32[4096]{0:T(1024)S(1)}, s32[4096]{0:T(1024)}, u32[]{:S(2)}) copy-start(s32[4096]{0:T(1024)} %param.17) | copy-start | bytes 49156
  0.6 0.7 %copy-start.10 = (s32[1,1,16,1]{2,3,1,0:T(1,128)S(1)}, s32[1,1,16,1]{2,3,1,0:T(1,128)}, u32[]{:S(2)}) copy-start(s32[1,1,16,1]{2,3,1,0:T(1,128)} %param.20) | copy-start | bytes 196
  0.7 0.7 %copy-start.5 = (f32[2000]{0:T(1024)S(1)}, f32[2000]{0:T(1024)}, u32[]{:S(2)}) copy-start(f32[2000]{0:T(1024)} %param.13) | copy-start | bytes 24004
  1.3 0.7 %copy-start.9 = (f32[48]{0:T(128)S(1)}, f32[48]{0:T(128)}, u32[]{:S(2)}) copy-start(f32[48]{0:T(128)} %param.12) | copy-start | bytes 580
  2.0 1.2 %copy-start = (f32[124,1,1,1,16,128]{5,4,3,2,1,0:T(8,128)S(1)}, f32[124,1,1,1,16,128]{5,4,3,2,1,0:T(8,128)}, u32[]{:S(2)}) copy-start(f32[124,1,1,1,16,128]{5,4,3,2,1,0:T(8,128)} %param.21) | copy-start | bytes 3047428
  3.2 1.0 %copy-start.1 = (f32[4,16,16,128]{3,2,1,0:T(8,128)S(1)}, f32[4,16,16,128]{3,2,1,0:T(8,128)}, u32[]{:S(2)}) copy-start(f32[4,16,16,128]{3,2,1,0:T(8,128)} %param.11) | copy-start | bytes 1572868
  4.2 0.8 %copy-start.2 = (s32[3,4096]{1,0:T(4,128)S(1)}, s32[3,4096]{1,0:T(4,128)}, u32[]{:S(2)}) copy-start(s32[3,4096]{1,0:T(4,128)} %spos_r.1) | copy-start | bytes 147460
  5.1 0.7 %copy-start.4 = (f32[4096]{0:T(1024)S(1)}, f32[4096]{0:T(1024)}, u32[]{:S(2)}) copy-start(f32[4096]{0:T(1024)} %param.18) | copy-start | bytes 49156
  5.8 0.7 %copy-start.6 = (f32[2000]{0:T(1024)S(1)}, f32[2000]{0:T(1024)}, u32[]{:S(2)}) copy-start(f32[2000]{0:T(1024)} %param.14) | copy-start | bytes 24004
  6.5 0.7 %copy-start.7 = (s32[2000]{0:T(1024)S(1)}, s32[2000]{0:T(1024)}, u32[]{:S(2)}) copy-start(s32[2000]{0:T(1024)} %param.15) | copy-start | bytes 24004
  7.2 0.7 %copy-start.8 = (s32[1,1,1,16,128]{4,3,2,1,0:T(8,128)S(1)}, s32[1,1,1,16,128]{4,3,2,1,0:T(8,128)}, u32[]{:S(2)}) copy-start(s32[1,1,1,16,128]{4,3,2,1,0:T(8,128)} %param.19) | copy-start | bytes 24580

commit v2 on v1

--- a/solution.py
+++ b/solution.py
@@ -215,7 +215,9 @@
     for n in range(STEPS):
         bt[n * NB:(n + 1) * NB, :] = jnp.broadcast_to(basis[:, HIST + n:HIST + n + 1], (NB, CAP))
 
-    live = jnp.where(lane < count_r[...], 1.0, 0.0).astype(F32)
+    held = iota((OWN, OWN), 0) == iota((OWN, OWN), 1)
+    counts = jnp.sum(jnp.where(held, count_r[...].astype(F32), 0.0), axis=1, keepdims=True)
+    live = jnp.where(lane.astype(F32) < counts, 1.0, 0.0).astype(F32)
     hist_load.wait()
     hv[HIST * OWN:, :] = jnp.zeros((STEPS * OWN, CAP), F32)
     bh, bl = split(basis)
@@ -436,7 +438,7 @@
             pltpu.SemaphoreType.DMA((OWN,)),
         ],
         compiler_params=pltpu.CompilerParams(
-            collective_id=0, has_side_effects=True, vmem_limit_bytes=40 * 1024 * 1024
+            collective_id=0, has_side_effects=True, vmem_limit_bytes=63 * 1024 * 1024
         ),
     )(
         fields.reshape(4, ROWS, TZ),
@@ -448,7 +450,7 @@
         src_id.reshape(1, SRC),
         src_gain.reshape(1, SRC),
         sample_cell.reshape(OWN, CAP),
-        sample_count.reshape(OWN, 1),
+        sample_count.reshape(1, OWN),
         history.reshape(HIST * OWN, CAP),
     )
     return fields_out.reshape(fields.shape), coefficients.reshape(NB, 1, 1, 1, OWN, CAP)

time: 50.4 us -> 43.4 us (0.86)
  local copies, waits for them, and re-layouts: 8.88 us -> 2.82 us
  Pallas kernels: 40.4 us -> 39.8 us
    unnamed x24 -> x4, local copies, waits for them, and re-layouts: 8.79 us -> 2.82 us
    pallas_call x1, Pallas kernels: 40.4 us -> 39.8 us  [body(): pl.pallas_call(kernel, out_shape=(jax.ShapeDtypeStruct((4, ROWS, TZ), F32...]
where the time goes in v2:
time: 43.4 us; the launch traced here: 43.2 us
  Pallas kernels  39.8 us (92%)
  local copies, waits for them, and re-layouts  2.82 us (6%)
  between operations  0.65 us (1%)
    pallas_call x1, Pallas kernels, body(): pl.pallas_call(kernel, out_shape=(jax.ShapeDtypeStruct((4, ROWS, TZ), F32...  39.8 us
    unnamed x4, local copies, waits for them, and re-layouts  2.82 us

profile of v2, /device:TPU:1, one launch (start us, length us, event | category | flops | bytes accessed | tf_op | source)
XLA Modules:
  0.0 43.2 jit_solution(11794708877220751146)
XLA Ops:
  0.6 39.8 %shard_map.122 = (f32[4,256,128]{2,1,0:T(8,128)}, f32[1536,128]{1,0:T(8,128)}) custom-call(f32[4,256,128]{2,1,0:T(8,128)} %bitcast.16, f32[1,48]{1,0:T(1,128)} %bitcast.24, f32[1,2000]{1,0:T(1,128)} %bitcast.20, f32[1,2000]{1,0:T(1,128)} %bitcast.21, s32[1,2000]{1,0:T(1,128)} %bitcast.22, s32[3,4096]{1,0:T(4,128)} %spos_r.1, s32[1,4096]{1,0:T(1,128)} %bitcast.18, ...), custom_call_target="tpu_custom_call" | custom-call | tf_op jit(solution)/shard_map/pallas_call | solution.py:394
  40.4 0.0 copy-start
  40.4 1.9 %copy.16 = f32[4,16,16,128]{3,2,1,0:T(8,128)} copy(f32[4,16,16,128]{3,2,1,0:T(8,128)} %bitcast.17) | data formatting | bytes 1048576
  42.4 0.0 copy-done
  42.4 0.9 %copy.17 = f32[96,1,1,1,16,128]{5,4,3,2,1,0:T(8,128)} copy(f32[96,1,1,1,16,128]{5,4,3,2,1,0:T(8,128)S(1)} %bitcast.15) | data formatting | bytes 1572864
Async XLA Ops:
  40.4 2.0 %copy-start = (f32[1536,128]{1,0:T(8,128)S(1)}, f32[1536,128]{1,0:T(8,128)}, u32[]{:S(2)}) copy-start(f32[1536,128]{1,0:T(8,128)} %get-tuple-element.5) | copy-start | bytes 2359300

commit v3 on v2

v3 whole, which is shorter than its diff:
```python
import jax
import jax.numpy as jnp
from jax import lax
from jax.experimental import pallas as pl
from jax.experimental.pallas import tpu as pltpu
from jax.sharding import PartitionSpec as P

STEPS = 4
HIST = 124
SOURCES = 48
TONES = 48
MODES = 2000
SRC = 4096
TX, TY, TZ = 16, 16, 128
ROWS = TX * TY
OWN = 16
CAP = 128
SLOTS = OWN * CAP
NB = 2 * TONES
KC = 1024
F32 = jnp.float32
BF = jnp.bfloat16
MESH = pl.DeviceIdType.MESH


def split(values):
    high = values.astype(BF)
    return high, (values - high.astype(F32)).astype(BF)


def dot_nn(a, b):
    return lax.dot_general(a, b, (((1,), (0,)), ((), ())), preferred_element_type=F32)


def dot_nt(a, b):
    return lax.dot_general(a, b, (((1,), (1,)), ((), ())), preferred_element_type=F32)


def half_wave(x, half):
    k = jnp.floor(x * 0.3183098861837907 + (0.5 - half))
    h = k + half
    r = x - h * 3.140625
    r = r - h * 0.0009670257568359375
    r = r - h * 6.2771141529083251953e-07
    q = r * r
    s = -2.505210838544172e-08
    for c in (2.7557319223985893e-06, -1.984126984126984e-04, 8.333333333333333e-03, -0.16666666666666666):
        s = s * q + c
    s = r + r * q * s
    sign = 1.0 - 2.0 * (k - 2.0 * jnp.floor(k * 0.5))
    return jnp.where(half > 0.25, -sign, sign) * s


def iota(shape, dim):
    return lax.broadcasted_iota(jnp.int32, shape, dim)


GROUP = 8
WIDE = 24
EXT = 584
WIDTHS = (("p", 4), ("c", 3), ("v", 3), ("d2", 2), ("d3", 1))
PLANES = [(f, k) for f, width in WIDTHS for k in range(width)]
DIAGS = ((-1, -1), (-1, 1), (1, -1), (1, 1))
SIDES = ((-1, 0), (1, 0), (0, -1), (0, 1)) + DIAGS
CORNER = [("p", i, j) for i in range(3) for j in range(3 - i)] + [
    (f, i, j) for f in ("c", "v") for i in range(2) for j in range(2 - i)] + [("d2", 0, 0)]
ZPACK = (("p", 4, 65), ("c", 4, 65), ("d2", 10, 53), ("d3", 13, 47))


def row_of(x, y):
    return 8 + WIDE * (x + 4) + y


def zpack_slots():
    start, at = {}, 0
    for f, first, count in ZPACK:
        start[f] = at
        at += -(-count // 16)
    return start, at


ZSTART, ZCOUNT = zpack_slots()


def roll_lanes(v, by):
    return pltpu.roll(v, by % TZ, 1) if by % TZ else v


def kernel(
    fields_h, tone_r, mfreq_r, mamp_r, mmap_r, spos_r, sid_r, sgain_r, cell_r, count_r, hist_h,
    fout_h, cout_h,
    fv, hv, pm, pq, cm, cq, d2m, d2q, d3m, d3q, d4, vzm, vxs, vys, plast, sm, sq,
    ms, wv, srow, scol, acc, cone, rsel, ov, bt, sb, rb,
    xs, xr, ys, yr, ds, dr, zs, zr,
    fsem, hsem, osem, ss, rs, zss, zrs, ass, ars,
):
    ix = lax.axis_index("gx")
    iy = lax.axis_index("gy")
    iz = lax.axis_index("gz")
    low_x, high_x = ix == 0, ix == 3
    low_y, high_y = iy == 0, iy == 3
    low_z, high_z = iz == 0, iz == OWN - 1

    loads = [pltpu.make_async_copy(fields_h.at[k], fv.at[k], fsem.at[k]) for k in range(4)]
    for copy in loads:
        copy.start()
    hist_load = pltpu.make_async_copy(hist_h, hv.at[pl.ds(0, HIST * OWN)], hsem)
    hist_load.start()

    def has(sx, sy):
        ok = None
        for s, low, high in ((sx, low_x, high_x), (sy, low_y, high_y)):
            if s:
                here = jnp.logical_not(low if s < 0 else high)
                ok = here if ok is None else ok & here
        return ok

    def at_side(sx, sy):
        where = {}
        if sx:
            where["gx"] = ix + sx
        if sy:
            where["gy"] = iy + sy
        return where

    barrier = pltpu.get_barrier_semaphore()
    for k in range(1, OWN):
        pl.semaphore_signal(barrier, inc=1, device_id={"gz": lax.rem(iz + k, OWN)}, device_id_type=MESH)
    expected = OWN - 1
    for side in SIDES:
        expected = expected + jnp.where(has(*side), 1, 0)

        @pl.when(has(*side))
        def _(side=side):
            pl.semaphore_signal(barrier, inc=1, device_id=at_side(*side), device_id_type=MESH)

    lane = iota((1, TZ), 1)
    sub = iota((TY, 1), 0)
    row8 = iota((8, 1), 0)
    ext = {"p": pm.at[0], "c": cm, "v": vzm, "d2": d2m, "d3": d3m}
    ring = {"p": pq.at[0], "c": cq, "d2": d2q, "d3": d3q}
    for ref in (cm, cq, d2m, d2q, d3m, d3q, vzm, vxs, vys, sm, sq, pm, pq):
        ref[...] = jnp.zeros_like(ref)

    ms[...] = jnp.zeros_like(ms)
    ms[0:1, 0:MODES] = mfreq_r[...]
    ms[1:2, 0:MODES] = mamp_r[...]
    ms[2:3, 0:MODES] = mmap_r[...].astype(F32)
    moment = (HIST + row8 % STEPS).astype(F32)
    waves = ms[1:2, :] * half_wave(ms[0:1, :] * moment, jnp.zeros((8, 1), F32))
    high = waves.astype(BF).astype(F32)
    waves = jnp.where(row8 < STEPS, high, waves - high).astype(BF)
    pick = jnp.where(iota((SOURCES, 1), 0).astype(F32) == ms[2:3, :], 1.0, 0.0).astype(BF)
    drive = dot_nt(waves, pick)
    drive = drive + pltpu.roll(drive, 4, 0)
    high = drive.astype(BF).astype(F32)
    drive = jnp.where(row8 < STEPS, high, drive - high).astype(BF)
    pick = jnp.where(iota((SOURCES, 1), 0) == sid_r[...], 1.0, 0.0).astype(BF)
    weight = dot_nn(drive, pick)
    weight = (weight + pltpu.roll(weight, 4, 0)) * sgain_r[...]
    high = weight.astype(BF).astype(F32)
    wv[...] = jnp.where(row8 < STEPS, high, weight - high)
    lx = spos_r[0:1, :] - ix * TX
    ly = spos_r[1:2, :] - iy * TY
    lz = spos_r[2:3, :] - iz * TZ
    inside = (lx >= 0) & (lx < TX) & (ly >= 0) & (ly < TY) & (lz >= 0) & (lz < TZ)
    srow[...] = jnp.where(inside, lx * TY + ly, -1).astype(F32)
    scol[...] = lz.astype(F32)

    acc[...] = jnp.zeros_like(acc)

    @pl.loop(0, SRC // KC)
    def _(chunk):
        span = pl.ds(pl.multiple_of(chunk * KC, KC), KC)
        a = jnp.where(iota((ROWS, 1), 0).astype(F32) == srow[:, span], 1.0, 0.0).astype(BF)
        m = iota((TZ, 1), 0).astype(F32) == scol[:, span]
        b = jnp.concatenate([jnp.where(m, wv[q:q + 1, span], 0.0).astype(BF) for q in range(2 * STEPS)], axis=0)
        acc[...] += dot_nt(a, b)

    for copy in loads:
        copy.wait()
    for x in range(TX):
        at = slice(x * TY, (x + 1) * TY)
        to = slice(row_of(x, 0), row_of(x, 0) + TY)
        added = [acc[at, n * TZ:(n + 1) * TZ] + acc[at, (STEPS + n) * TZ:(STEPS + n + 1) * TZ] for n in range(STEPS)]
        p = fv[0, at, :]
        vx, vy, vz = (fv[k, at, :] for k in (1, 2, 3))
        gone = vx + (vy - jnp.where(sub == 0, 0.0, pltpu.roll(vy, 1, 0)))
        gone = gone + (vz - jnp.where(lane == 0, 0.0, pltpu.roll(vz, 1, 1)))
        if x:
            gone = gone - fv[1, (x - 1) * TY:x * TY, :]
        pm[0, to, :] = p
        cm[to, :] = added[0] - 0.5 * (gone + p)
        d2m[to, :] = added[1] - added[0]
        d3m[to, :] = added[2] - added[1]
        d4[at, :] = added[3] - added[2]
        vzm[to, :] = 0.5 * vz
    vxs[1, 4:20, :] = 0.5 * fv[1, ROWS - TY:ROWS, :]
    vys[1, 4:20, :] = 0.5 * fv[2, pl.ds(TY - 1, TX, stride=TY), :]

    for s in (0, 1):
        cell = (lambda k: k) if s == 0 else (lambda k: TX - 1 - k)
        for i, (f, k) in enumerate(PLANES):
            xs[s, i * 16:(i + 1) * 16, :] = ext[f][row_of(cell(k), 0):row_of(cell(k), 0) + TY, :]
            ys[s, i * 16:(i + 1) * 16, :] = ext[f][pl.ds(row_of(0, cell(k)), TX, stride=WIDE), :]
        for k in range(3):
            xs[s, 208 + k:209 + k, :] = vys[1, 4 + cell(k):5 + cell(k), :]
            ys[s, 208 + k:209 + k, :] = vxs[1, 4 + cell(k):5 + cell(k), :]
    xs[1, 224:240, :] = vxs[1, 4:20, :]
    ys[1, 224:240, :] = vys[1, 4:20, :]
    for s, (sx, sy) in enumerate(DIAGS):
        cx = (lambda k: k) if sx < 0 else (lambda k: TX - 1 - k)
        cy = (lambda k: k) if sy < 0 else (lambda k: TY - 1 - k)
        for i, (f, a, b) in enumerate(CORNER):
            r = row_of(cx(a), cy(b))
            ds[s, i:i + 1, :] = ext[f][r:r + 1, :]
        for k in range(3):
            ds[s, 13 + k:14 + k, :] = vxs[1, 4 + cy(k):5 + cy(k), :]
            ds[s, 16 + k:17 + k, :] = vys[1, 4 + cx(k):5 + cx(k), :]

    eye = iota((TONES, TONES), 0) == iota((TONES, TONES), 1)
    freq = jnp.sum(jnp.where(eye, tone_r[...], 0.0), axis=1, keepdims=True)
    freq = jnp.concatenate([freq, freq], axis=0)
    angle = freq * lane.astype(F32)
    basis = half_wave(angle, jnp.where(iota((NB, 1), 0) < TONES, 0.5, 0.0).astype(F32)) * 0.125
    for n in range(STEPS):
        bt[n * NB:(n + 1) * NB, :] = jnp.broadcast_to(basis[:, HIST + n:HIST + n + 1], (NB, CAP))
    held = iota((OWN, OWN), 0) == iota((OWN, OWN), 1)
    counts = jnp.sum(jnp.where(held, count_r[...].astype(F32), 0.0), axis=1, keepdims=True)
    live = jnp.where(lane.astype(F32) < counts, 1.0, 0.0).astype(F32)
    hist_load.wait()
    hv[HIST * OWN:, :] = jnp.zeros((STEPS * OWN, CAP), F32)
    bh, bl = split(basis)
    lhs = jnp.concatenate([bh, bl, bh], axis=1)
    for e in range(0, OWN, 2):
        hh, hl = split(jnp.concatenate(
            [hv[pl.ds(e, HIST + STEPS, stride=OWN), :], hv[pl.ds(e + 1, HIST + STEPS, stride=OWN), :]], axis=1))
        part = dot_nn(lhs, jnp.concatenate([hh, hh, hl], axis=0))
        ov[pl.ds(e, NB, stride=OWN), :] = part[:, :CAP] * live[e:e + 1]
        ov[pl.ds(e + 1, NB, stride=OWN), :] = part[:, CAP:] * live[e + 1:e + 2]

    for d in range(OWN):
        cells = cell_r[d:d + 1, :]
        span = slice(d * CAP, (d + 1) * CAP)
        one = jnp.where(iota((TZ, 1), 0) == cells % TZ, 1.0, 0.0).astype(BF)
        cone[0:TZ, span] = one
        cone[TZ:2 * TZ, span] = one
        rsel[:, span] = cells // TZ
    sb[...] = jnp.zeros_like(sb)

    def first_copies():
        made = []
        for i, side in enumerate(SIDES):
            if i < 2:
                src, dst, rows = xs.at[i], xr.at[i], 224 + 16 * i
            elif i < 4:
                src, dst, rows = ys.at[i - 2], yr.at[i - 2], 224 + 16 * (i - 2)
            else:
                src, dst, rows = ds.at[i - 4], dr.at[i - 4], 24
            made.append(pltpu.make_async_remote_copy(
                src_ref=src.at[pl.ds(0, rows)], dst_ref=dst.at[pl.ds(0, rows)], send_sem=ss.at[i], recv_sem=rs.at[i],
                device_id=at_side(*side), device_id_type=MESH))
        return made

    firsts = first_copies()
    pl.semaphore_wait(barrier, expected)
    for side, copy in zip(SIDES, firsts):
        @pl.when(has(*side))
        def _(copy=copy):
            copy.start()

    for i in range(4):
        sx, sy = SIDES[i]
        s = i % 2
        out = (lambda k: TX + k) if s == 0 else (lambda k: -1 - k)

        @pl.when(has(-sx, -sy))
        def _(i=i, s=s, out=out):
            firsts[i].wait_recv()
            for j, (f, k) in enumerate(PLANES):
                if i < 2:
                    ext[f][row_of(out(k), 0):row_of(out(k), 0) + TY, :] = xr[s, j * 16:(j + 1) * 16, :]
                else:
                    ext[f][pl.ds(row_of(0, out(k)), TX, stride=WIDE), :] = yr[s, j * 16:(j + 1) * 16, :]
            got = xr if i < 2 else yr
            side_v, low_v = (vys, vxs) if i < 2 else (vxs, vys)
            for k in range(3):
                side_v[1, 4 + out(k):5 + out(k), :] = got[s, 208 + k:209 + k, :]
            if s == 1:
                low_v[0, 4:20, :] = got[s, 224:240, :]

    for i in range(4, 8):
        sx, sy = SIDES[i]
        ox = (lambda k: TX + k) if sx < 0 else (lambda k: -1 - k)
        oy = (lambda k: TY + k) if sy < 0 else (lambda k: -1 - k)

        @pl.when(has(-sx, -sy))
        def _(i=i, sx=sx, sy=sy, ox=ox, oy=oy):
            firsts[i].wait_recv()
            for j, (f, a, b) in enumerate(CORNER):
                r = row_of(ox(a), oy(b))
                ext[f][r:r + 1, :] = dr[i - 4, j:j + 1, :]
            for k in range(3):
                if sx > 0:
                    vxs[0, 4 + oy(k):5 + oy(k), :] = dr[i - 4, 13 + k:14 + k, :]
                if sy > 0:
                    vys[0, 4 + ox(k):5 + ox(k), :] = dr[i - 4, 16 + k:17 + k, :]

    for k, x in ((0, 0), (1, TX)):
        r = row_of(x, -4)
        cm[r:r + WIDE, :] = cm[r:r + WIDE, :] + vxs[k]
    for k, y in ((0, 0), (1, TY)):
        r = pl.ds(row_of(-4, y), WIDE, stride=WIDE)
        cm[r, :] = cm[r, :] + vys[k]

    for flag, low, along_x in ((low_x, True, True), (high_x, False, True), (low_y, True, False), (high_y, False, False)):
        @pl.when(flag)
        def _(low=low, along_x=along_x):
            def rows(q):
                return pl.ds(row_of(q, -4), WIDE) if along_x else pl.ds(row_of(-4, q), WIDE, stride=WIDE)

            for f, width in WIDTHS:
                for k in range(width):
                    if low:
                        ext[f][rows(-1 - k), :] = ext[f][rows(k), :]
                    elif k == 0:
                        ext[f][rows(TX), :] = jnp.zeros((WIDE, TZ), F32)
                    else:
                        ext[f][rows(TX + k), :] = -ext[f][rows(TX - k), :]

    for f, first, count in ZPACK:
        for t in range(0, count, 16):
            packed = jnp.zeros((GROUP, TZ), F32)
            for u in range(min(16, count - t)):
                g = first + t + u
                value = ext[f][g * 8:g * 8 + 8, :]
                if f == "c":
                    value = jnp.where(lane == TZ - 4, roll_lanes(vzm[g * 8:g * 8 + 8, :], -3), value)
                here = ((lane + 4) % TZ) // 8 == u
                packed = jnp.where(here, roll_lanes(value, 8 * u), packed)
            zs[ZSTART[f] + t // 16] = packed

    to_z = [
        pltpu.make_async_remote_copy(
            src_ref=zs, dst_ref=zr.at[s], send_sem=zss.at[s], recv_sem=zrs.at[s],
            device_id={"gz": iz + (2 * s - 1)}, device_id_type=MESH)
        for s in (0, 1)
    ]
    from_z = (jnp.logical_not(high_z), jnp.logical_not(low_z))
    for s in (0, 1):
        @pl.when(from_z[1 - s])
        def _(s=s):
            to_z[s].start()
    for s in (0, 1):
        @pl.when(from_z[s])
        def _(s=s):
            to_z[s].wait_recv()

    place = (lane + 4) % 8
    for f, first, count in ZPACK:
        for t in range(0, count, 16):
            slot = ZSTART[f] + t // 16
            own = zs[slot]
            below = jnp.zeros((GROUP, TZ), F32)
            above = jnp.zeros((GROUP, TZ), F32)
            for k in range(4):
                if not (f == "c" and k == 3):
                    below = jnp.where(place == 3 - k, roll_lanes(own, -(2 * k + 1)), below)
                if k:
                    above = jnp.where(place == 4 + k, -roll_lanes(own, 2 * k), above)
            merged = jnp.where(
                place < 4, jnp.where(low_z, below, zr[1, slot]), jnp.where(high_z, above, zr[0, slot]))
            for u in range(min(16, count - t)):
                g = first + t + u
                at = slice(g * 8, g * 8 + 8)
                value = roll_lanes(merged, -8 * u)
                if f == "c":
                    flow = roll_lanes(jnp.where(lane == TZ - 4, value, 0.0), 4)
                    cm[at, :] = cm[at, :] + flow
                    flow = roll_lanes(jnp.where(lane == TZ - 1, vzm[at, :], 0.0), 1)
                    value = value + jnp.where(high_z, 0.0, flow)
                ring[f][at, :] = value

    def listen(n, get):
        lhs = jnp.concatenate(split(get), axis=1)
        for d in range(0, OWN, 2):
            span = slice(d * CAP, (d + 2) * CAP)
            seen = dot_nn(lhs, cone[:, span])
            got = jnp.sum(jnp.where(iota((ROWS, 1), 0) == rsel[:, span], seen, 0.0), axis=0, keepdims=True)
            sb[d * 8 + n:d * 8 + n + 1, :] = got[:, :CAP]
            sb[(d + 1) * 8 + n:(d + 1) * 8 + n + 1, :] = got[:, CAP:]

    for n in range(STEPS):
        d_main = (cm, d2m, d3m, d4)[n]
        d_ring = (cq, d2q, d3q, None)[n]
        main_span = (range(4, 69), range(7, 66), range(10, 63), [g for g in range(13, 60) if g % 3])[n]
        ring_span = (range(7, 66), range(10, 63), range(13, 60), ())[n]
        for g in main_span:
            at = slice(g * 8, g * 8 + 8)
            here, ghost = pm[n, at, :], pq[n, at, :]

            def stepped(ref, d, here, other):
                sums = (ref[n, g * 8 - WIDE:g * 8 - WIDE + 8, :] + ref[n, g * 8 + WIDE:g * 8 + WIDE + 8, :]) + (
                    ref[n, g * 8 - 1:g * 8 + 7, :] + ref[n, g * 8 + 1:g * 8 + 9, :])
                back = pltpu.roll(jnp.where(lane == TZ - 1, other, here), 1, 1)
                fore = pltpu.roll(jnp.where(lane == 0, other, here), TZ - 1, 1)
                new = d + 0.25 * (sums + (back + fore))
                return new if n == 0 else new + (0.5 * here - ref[n - 1, at, :])

            if n < STEPS - 1:
                pm[n + 1, at, :] = stepped(pm, d_main[at, :], here, ghost)
                if g in ring_span:
                    pq[n + 1, at, :] = stepped(pq, d_ring[at, :], ghost, here)
            else:
                x, half = divmod(g - 13, 3)
                own = slice(x * TY + half * 8, x * TY + half * 8 + 8)
                plast[own, :] = stepped(pm, d4[own, :], here, ghost)
        if n < STEPS - 1:
            listen(n, jnp.concatenate([pm[n + 1, row_of(x, 0):row_of(x, 0) + TY, :] for x in range(TX)], axis=0))
        else:
            listen(n, plast[...])

    def block_copy(k):
        target = lax.rem(iz + k, OWN)
        return pltpu.make_async_remote_copy(
            src_ref=sb.at[pl.ds(pl.multiple_of(target * 8, 8), 8)],
            dst_ref=rb.at[pl.ds(pl.multiple_of(iz * 8, 8), 8)],
            send_sem=ass.at[k], recv_sem=ars.at[k], device_id={"gz": target}, device_id_type=MESH)

    sends = [block_copy(k) for k in range(1, OWN)]
    for k in (8, 7, 9, 6, 10, 5, 11, 4, 12, 3, 13, 2, 14, 1, 15):
        sends[k - 1].start()
    mine = pl.ds(pl.multiple_of(iz * 8, 8), 8)
    rb[mine, :] = sb[mine, :]

    outs = [pltpu.make_async_copy(plast, fout_h.at[0], osem.at[0])]
    outs[0].start()
    for side, copy in zip(SIDES, firsts):
        @pl.when(has(*side))
        def _(copy=copy):
            copy.wait_send()
    for s in (0, 1):
        @pl.when(from_z[1 - s])
        def _(s=s):
            to_z[s].wait_send()
    for g in range(13, 64):
        at = slice(g * 8, g * 8 + 8)
        sm[at, :] = (pm[0, at, :] + pm[1, at, :]) + (pm[2, at, :] + pm[3, at, :])
        sq[at, :] = (pq[0, at, :] + pq[1, at, :]) + (pq[2, at, :] + pq[3, at, :])
    for x in range(TX):
        at = slice(x * TY, (x + 1) * TY)
        r = row_of(x, 0)
        own = sm[r:r + TY, :]
        fv[1, at, :] = fv[1, at, :] - 0.5 * (sm[r + WIDE:r + WIDE + TY, :] - own)
        fv[2, at, :] = fv[2, at, :] - 0.5 * (sm[r + 1:r + 1 + TY, :] - own)
        fore = pltpu.roll(jnp.where(lane == 0, sq[r:r + TY, :], own), TZ - 1, 1)
        fv[3, at, :] = fv[3, at, :] - 0.5 * (fore - own)
    outs.append(pltpu.make_async_copy(fv.at[pl.ds(1, 3)], fout_h.at[pl.ds(1, 3)], osem.at[1]))
    outs[1].start()

    for copy in sends:
        copy.wait_recv()
    heard = [rb[pl.ds(n, OWN, stride=8), :] * live for n in range(STEPS)]
    parts = 4
    per = NB // parts
    for part in range(parts):
        for j in range(part * per, (part + 1) * per):
            at = slice(j * OWN, (j + 1) * OWN)
            term = ov[at, :]
            for n in range(STEPS):
                term = term + bt[n * NB + j:n * NB + j + 1, :] * heard[n]
            ov[at, :] = term
        rows = pl.ds(part * per * OWN, per * OWN)
        outs.append(pltpu.make_async_copy(ov.at[rows], cout_h.at[rows], osem.at[2 + part]))
        outs[-1].start()
    for copy in sends:
        copy.wait_send()
    for copy in outs:
        copy.wait()


def body(
    fields, tone_freq, mode_freq, mode_amp, mode_map, src_pos, src_id, src_gain, sample_cell, sample_count, history
):
    vmem = pl.BlockSpec(memory_space=pltpu.VMEM)
    hbm = pl.BlockSpec(memory_space=pl.ANY)
    face = (STEPS, TY, TZ)
    fields_out, coefficients = pl.pallas_call(
        kernel,
        out_shape=(
            jax.ShapeDtypeStruct((4, ROWS, TZ), F32),
            jax.ShapeDtypeStruct((NB * OWN, CAP), F32),
        ),
        in_specs=[hbm] + [vmem] * 9 + [hbm],
        out_specs=(hbm, hbm),
        scratch_shapes=[
            pltpu.VMEM((4, ROWS, TZ), F32),
            pltpu.VMEM(((HIST + STEPS) * OWN, CAP), F32),
            pltpu.VMEM((STEPS, EXT, TZ), F32),
            pltpu.VMEM((STEPS, EXT, TZ), F32),
            pltpu.VMEM((EXT, TZ), F32),
            pltpu.VMEM((EXT, TZ), F32),
            pltpu.VMEM((EXT, TZ), F32),
            pltpu.VMEM((EXT, TZ), F32),
            pltpu.VMEM((EXT, TZ), F32),
            pltpu.VMEM((EXT, TZ), F32),
            pltpu.VMEM((ROWS, TZ), F32),
            pltpu.VMEM((EXT, TZ), F32),
            pltpu.VMEM((2, WIDE, TZ), F32),
            pltpu.VMEM((2, WIDE, TZ), F32),
            pltpu.VMEM((ROWS, TZ), F32),
            pltpu.VMEM((EXT, TZ), F32),
            pltpu.VMEM((EXT, TZ), F32),
            pltpu.VMEM((8, 2048), F32),
            pltpu.VMEM((8, SRC), F32),
            pltpu.VMEM((1, SRC), F32),
            pltpu.VMEM((1, SRC), F32),
            pltpu.VMEM((ROWS, 2 * STEPS * TZ), F32),
            pltpu.VMEM((2 * TZ, SLOTS), BF),
            pltpu.VMEM((1, SLOTS), jnp.int32),
            pltpu.VMEM((NB * OWN, CAP), F32),
            pltpu.VMEM((STEPS * NB, CAP), F32),
            pltpu.VMEM((OWN * 8, CAP), F32),
            pltpu.VMEM((OWN * 8, CAP), F32),
            pltpu.VMEM((2, 240, TZ), F32),
            pltpu.VMEM((2, 240, TZ), F32),
            pltpu.VMEM((2, 240, TZ), F32),
            pltpu.VMEM((2, 240, TZ), F32),
            pltpu.VMEM((4, 24, TZ), F32),
            pltpu.VMEM((4, 24, TZ), F32),
            pltpu.VMEM((ZCOUNT, GROUP, TZ), F32),
            pltpu.VMEM((2, ZCOUNT, GROUP, TZ), F32),
            pltpu.SemaphoreType.DMA((4,)),
            pltpu.SemaphoreType.DMA,
            pltpu.SemaphoreType.DMA((6,)),
            pltpu.SemaphoreType.DMA((8,)),
            pltpu.SemaphoreType.DMA((8,)),
            pltpu.SemaphoreType.DMA((2,)),
            pltpu.SemaphoreType.DMA((2,)),
            pltpu.SemaphoreType.DMA((OWN,)),
            pltpu.SemaphoreType.DMA((OWN,)),
        ],
        compiler_params=pltpu.CompilerParams(
            collective_id=0, has_side_effects=True, vmem_limit_bytes=63 * 1024 * 1024
        ),
    )(
        fields.reshape(4, ROWS, TZ),
        tone_freq.reshape(1, TONES),
        mode_freq.reshape(1, MODES),
        mode_amp.reshape(1, MODES),
        mode_map.reshape(1, MODES),
        src_pos,
        src_id.reshape(1, SRC),
        src_gain.reshape(1, SRC),
        sample_cell.reshape(OWN, CAP),
        sample_count.reshape(1, OWN),
        history.reshape(HIST * OWN, CAP),
    )
    return fields_out.reshape(fields.shape), coefficients.reshape(NB, 1, 1, 1, OWN, CAP)


def solution(mesh):
    in_specs = (
        P(None, "gx", "gy", "gz"),
        P(),
        P(),
        P(),
        P(),
        P(),
        P(),
        P(),
        P("gx", "gy", "gz", None, None),
        P("gx", "gy", None, "gz"),
        P(None, "gx", "gy", "gz", None, None),
    )
    out_specs = (P(None, "gx", "gy", "gz"), P(None, "gx", "gy", "gz", None, None))
    return jax.shard_map(body, mesh=mesh, in_specs=in_specs, out_specs=out_specs, check_vma=False)
```

time: 43.4 us -> 36 us (0.83)
  Pallas kernels: 39.8 us -> 32.4 us
    pallas_call x1, Pallas kernels: 39.8 us -> 32.4 us  [body(): pl.pallas_call(kernel, out_shape=(jax.ShapeDtypeStruct((4, ROWS, TZ), F32...]
where the time goes in v3:
time: 36 us; the launch traced here: 35.9 us
  Pallas kernels  32.4 us (90%)
  local copies, waits for them, and re-layouts  2.82 us (8%)
  between operations  0.65 us (2%)
    pallas_call x1, Pallas kernels, body(): pl.pallas_call(kernel, out_shape=(jax.ShapeDtypeStruct((4, ROWS, TZ), F32...  32.4 us
    unnamed x4, local copies, waits for them, and re-layouts  2.82 us

profile of v3, /device:TPU:1, one launch (start us, length us, event | category | flops | bytes accessed | tf_op | source)
XLA Modules:
  0.0 35.9 jit_solution(7316077155745139035)
XLA Ops:
  0.6 32.4 %shard_map.122 = (f32[4,256,128]{2,1,0:T(8,128)}, f32[1536,128]{1,0:T(8,128)}) custom-call(f32[4,256,128]{2,1,0:T(8,128)} %bitcast.16, f32[1,48]{1,0:T(1,128)} %bitcast.24, f32[1,2000]{1,0:T(1,128)} %bitcast.20, f32[1,2000]{1,0:T(1,128)} %bitcast.21, s32[1,2000]{1,0:T(1,128)} %bitcast.22, s32[3,4096]{1,0:T(4,128)} %spos_r.1, s32[1,4096]{1,0:T(1,128)} %bitcast.18, ...), custom_call_target="tpu_custom_call" | custom-call | tf_op jit(solution)/shard_map/pallas_call | solution.py:488
  33.0 0.0 copy-start
  33.0 1.9 %copy.16 = f32[4,16,16,128]{3,2,1,0:T(8,128)} copy(f32[4,16,16,128]{3,2,1,0:T(8,128)} %bitcast.17) | data formatting | bytes 1048576
  35.0 0.0 copy-done
  35.0 0.9 %copy.17 = f32[96,1,1,1,16,128]{5,4,3,2,1,0:T(8,128)} copy(f32[96,1,1,1,16,128]{5,4,3,2,1,0:T(8,128)S(1)} %bitcast.15) | data formatting | bytes 1572864
Async XLA Ops:
  33.0 2.0 %copy-start = (f32[1536,128]{1,0:T(8,128)S(1)}, f32[1536,128]{1,0:T(8,128)}, u32[]{:S(2)}) copy-start(f32[1536,128]{1,0:T(8,128)} %get-tuple-element.5) | copy-start | bytes 2359300

commit v4 on v3

v4 whole, which is shorter than its diff:
```python
import jax
import jax.numpy as jnp
import numpy as np
from jax import lax
from jax.experimental import pallas as pl
from jax.experimental.pallas import tpu as pltpu
from jax.sharding import PartitionSpec as P

STEPS = 4
HIST = 124
SOURCES = 48
TONES = 48
MODES = 2000
SRC = 4096
TX, TY, TZ = 16, 16, 128
ROWS = TX * TY
OWN = 16
CAP = 128
SLOTS = OWN * CAP
NB = 2 * TONES
KC = 1024
F32 = jnp.float32
BF = jnp.bfloat16
MESH = pl.DeviceIdType.MESH
ONE = np.asarray(1, BF)
ZERO = np.asarray(0, BF)


def split(values):
    high = values.astype(BF)
    return high, (values - high.astype(F32)).astype(BF)


def dot_nn(a, b):
    return lax.dot_general(a, b, (((1,), (0,)), ((), ())), preferred_element_type=F32)


def dot_nt(a, b):
    return lax.dot_general(a, b, (((1,), (1,)), ((), ())), preferred_element_type=F32)


def half_wave(x, half):
    k = jnp.floor(x * 0.3183098861837907 + (0.5 - half))
    h = k + half
    r = x - h * 3.140625
    r = r - h * 0.0009670257568359375
    r = r - h * 6.2771141529083251953e-07
    q = r * r
    s = -2.505210838544172e-08
    for c in (2.7557319223985893e-06, -1.984126984126984e-04, 8.333333333333333e-03, -0.16666666666666666):
        s = s * q + c
    s = r + r * q * s
    sign = 1.0 - 2.0 * (k - 2.0 * jnp.floor(k * 0.5))
    return jnp.where(half > 0.25, -sign, sign) * s


def iota(shape, dim):
    return lax.broadcasted_iota(jnp.int32, shape, dim)


GROUP = 8
HALF = 8
BRIDGE = 3
WIDE = 24
EXT = 584
WIDTHS = (("p", 4), ("c", 3), ("d2", 2), ("d3", 1))
PLANES = [(f, k) for f, width in WIDTHS for k in range(width)]
RING_WIDTHS = (("p", 3), ("c", 2), ("d2", 1), ("v", 3))
RING_PLANES = [(f, k) for f, width in RING_WIDTHS for k in range(width)]
DIAGS = ((-1, -1), (-1, 1), (1, -1), (1, 1))
SIDES = ((-1, 0), (1, 0), (0, -1), (0, 1)) + DIAGS
CORNER = [("p", i, j) for i in range(3) for j in range(3 - i)] + [
    (f, i, j) for f in ("c", "v") for i in range(2) for j in range(2 - i)] + [("d2", 0, 0)]
RING_CORNER = [(f, i, j) for f in ("p", "v") for i in range(2) for j in range(2 - i)] + [("c", 0, 0)]
ALONG_Z = ("p", "c", "d2", "d3")
MAIN_GROUPS = [g for g in range(13, 60) if g % 3]


def row_of(x, y):
    return 8 + WIDE * (x + 4) + y


def roll_lanes(v, by):
    return pltpu.roll(v, by % TZ, 1) if by % TZ else v


def kernel(
    fields_h, tone_h, mfreq_h, mamp_h, mmap_h, spos_h, sid_h, sgain_h, cell_h, count_h, hist_h,
    fout_h, cout_h, heard_h, bt_h,
    tone_r, mfreq_r, mamp_r, mmap_r, spos_r, sid_r, sgain_r, cell_r, count_r,
    fv, hv, pm, pq, cm, cq, d2m, d2q, d3m, d3q, d4, vzm, vzq, vxs, vys, vxq, vyq, plast, sm, sq,
    ms, wv, srow, scol, acc, cone, zsel, both, ov, bt, sb, rb, hb,
    xs, xr, ys, yr, ds, dr, zs, zr, qs, qr, es, er, spare, zown,
    isem, fsem, hsem, osem, ss, rs, zss, zrs, qss, qrs, ass, ars, met, all_in,
):
    ix = lax.axis_index("gx")
    iy = lax.axis_index("gy")
    iz = lax.axis_index("gz")
    low_x, high_x = ix == 0, ix == 3
    low_y, high_y = iy == 0, iy == 3
    low_z, high_z = iz == 0, iz == OWN - 1

    def has(sx, sy):
        ok = None
        for s, low, high in ((sx, low_x, high_x), (sy, low_y, high_y)):
            if s:
                here = jnp.logical_not(low if s < 0 else high)
                ok = here if ok is None else ok & here
        return ok

    def at_side(sx, sy):
        where = {}
        if sx:
            where["gx"] = ix + sx
        if sy:
            where["gy"] = iy + sy
        return where

    barrier = pltpu.get_barrier_semaphore()
    half = (iz // HALF) * HALF
    bridge = (iz == BRIDGE) | (iz == BRIDGE + HALF)
    border = (iz == HALF - 1) | (iz == HALF)
    across = {"gz": lax.rem(iz + HALF, OWN)}
    mates = [{"gz": half + lax.rem(iz - half + k, HALF)} for k in range(1, HALF)]

    @pl.when(border)
    def _():
        pl.semaphore_signal(barrier, inc=1, device_id={"gz": OWN - 1 - iz}, device_id_type=MESH)

    @pl.when(bridge)
    def _():
        pl.semaphore_signal(barrier, inc=1, device_id=across, device_id_type=MESH)

    for mate in mates:
        pl.semaphore_signal(barrier, inc=1, device_id=mate, device_id_type=MESH)
    expected = HALF - 1 + jnp.where(border, 1, 0) + jnp.where(bridge, 1, 0)
    for side in SIDES:
        expected = expected + jnp.where(has(*side), 1, 0)

        @pl.when(has(*side))
        def _(side=side):
            pl.semaphore_signal(barrier, inc=1, device_id=at_side(*side), device_id_type=MESH)

    small = [
        pltpu.make_async_copy(src, dst, isem.at[k])
        for k, (src, dst) in enumerate((
            (mfreq_h, mfreq_r), (mamp_h, mamp_r), (mmap_h, mmap_r), (sid_h, sid_r), (sgain_h, sgain_r),
            (spos_h, spos_r), (tone_h, tone_r), (cell_h, cell_r), (count_h, count_r)))
    ]
    for copy in small:
        copy.start()
    loads = [pltpu.make_async_copy(fields_h.at[k], fv.at[k], fsem.at[k]) for k in range(4)]
    for copy in loads:
        copy.start()
    hist_load = pltpu.make_async_copy(hist_h, hv.at[pl.ds(0, HIST * OWN)], hsem)
    hist_load.start()

    lane = iota((1, TZ), 1)
    sub = iota((TY, 1), 0)
    row8 = iota((8, 1), 0)
    ext = {"p": pm.at[0], "c": cm, "v": vzm, "d2": d2m, "d3": d3m}
    ring = {"p": pq.at[0], "c": cq, "d2": d2q, "d3": d3q, "v": vzq}
    for ref in (vxs, vys, vxq, vyq, spare, sb):
        ref[...] = jnp.zeros_like(ref)

    ms[...] = jnp.zeros_like(ms)
    for copy in small:
        copy.wait()
    ms[0:1, 0:MODES] = mfreq_r[...]
    ms[1:2, 0:MODES] = mamp_r[...]
    ms[2:3, 0:MODES] = mmap_r[...].astype(F32)
    moment = (HIST + row8 % STEPS).astype(F32)
    waves = ms[1:2, :] * half_wave(ms[0:1, :] * moment, jnp.zeros((8, 1), F32))
    high = waves.astype(BF).astype(F32)
    waves = jnp.where(row8 < STEPS, high, waves - high).astype(BF)
    pick = jnp.where(iota((SOURCES, 1), 0).astype(F32) == ms[2:3, :], 1.0, 0.0).astype(BF)
    drive = dot_nt(waves, pick)
    drive = drive + pltpu.roll(drive, 4, 0)
    high = drive.astype(BF).astype(F32)
    drive = jnp.where(row8 < STEPS, high, drive - high).astype(BF)
    pick = jnp.where(iota((SOURCES, 1), 0) == sid_r[...], 1.0, 0.0).astype(BF)
    weight = dot_nn(drive, pick)
    weight = (weight + pltpu.roll(weight, 4, 0)) * sgain_r[...]
    high = weight.astype(BF).astype(F32)
    wv[...] = jnp.where(row8 < STEPS, high, weight - high)
    lx = spos_r[0:1, :] - ix * TX
    ly = spos_r[1:2, :] - iy * TY
    lz = spos_r[2:3, :] - iz * TZ
    inside = (lx >= 0) & (lx < TX) & (ly >= 0) & (ly < TY) & (lz >= 0) & (lz < TZ)
    srow[...] = jnp.where(inside, lx * TY + ly, -1).astype(F32)
    scol[...] = lz.astype(F32)

    def scattered(span):
        a = jnp.where(iota((ROWS, 1), 0).astype(F32).astype(BF) == srow[:, span].astype(BF), ONE, ZERO)
        m = iota((TZ, 1), 0).astype(F32).astype(BF) == scol[:, span].astype(BF)
        b = jnp.concatenate([jnp.where(m, wv[q:q + 1, span].astype(BF), ZERO) for q in range(2 * STEPS)], axis=0)
        return dot_nt(a, b)

    acc[...] = scattered(pl.ds(0, KC))

    @pl.loop(1, SRC // KC)
    def _(chunk):
        acc[...] += scattered(pl.ds(pl.multiple_of(chunk * KC, KC), KC))

    for copy in loads:
        copy.wait()
    for x in range(TX):
        at = slice(x * TY, (x + 1) * TY)
        to = slice(row_of(x, 0), row_of(x, 0) + TY)
        added = [acc[at, n * TZ:(n + 1) * TZ] + acc[at, (STEPS + n) * TZ:(STEPS + n + 1) * TZ] for n in range(STEPS)]
        p = fv[0, at, :]
        vx, vy, vz = (fv[k, at, :] for k in (1, 2, 3))
        gone = vx + (vy - jnp.where(sub == 0, 0.0, pltpu.roll(vy, 1, 0)))
        gone = gone + (vz - jnp.where(lane == 0, 0.0, pltpu.roll(vz, 1, 1)))
        if x:
            gone = gone - fv[1, (x - 1) * TY:x * TY, :]
        pm[0, to, :] = p
        cm[to, :] = added[0] - 0.5 * (gone + p)
        d2m[to, :] = added[1] - added[0]
        d3m[to, :] = added[2] - added[1]
        d4[at, :] = added[3] - added[2]
        vzm[to, :] = 0.5 * vz
    vxs[1, 4:20, :] = 0.5 * fv[1, ROWS - TY:ROWS, :]
    vys[1, 4:20, :] = 0.5 * fv[2, pl.ds(TY - 1, TX, stride=TY), :]

    def plane_at(along_x, q):
        return pl.ds(row_of(q, 0), TY) if along_x else pl.ds(row_of(0, q), TX, stride=WIDE)

    def inner(s):
        return (lambda k: k) if s == 0 else (lambda k: TX - 1 - k)

    def outer(s):
        return (lambda k: TX + k) if s == 0 else (lambda k: -1 - k)

    def up(step):
        return 0 if step < 0 else 1

    for face in range(4):
        along_x, s = face < 2, face % 2
        cell = inner(s)
        to = (xs if along_x else ys).at[s]
        for i, (f, k) in enumerate(PLANES):
            to[i * 16:(i + 1) * 16, :] = ext[f][plane_at(along_x, cell(k)), :]
        ends = jnp.zeros((TY, TZ), F32)
        for k in range(3):
            ends = jnp.where(lane == k, pltpu.roll(vzm[plane_at(along_x, cell(k)), :], k + 1, 1), ends)
        to[160:176, :] = ends
        beside, through = (vys, vxs) if along_x else (vxs, vys)
        for k in range(3):
            to[176 + k:177 + k, :] = beside[1, 4 + cell(k):5 + cell(k), :]
        if s == 1:
            to[192:208, :] = through[1, 4:20, :]
    for s, (sx, sy) in enumerate(DIAGS):
        cx, cy = inner(up(sx)), inner(up(sy))
        for i, (f, a, b) in enumerate(CORNER):
            r = row_of(cx(a), cy(b))
            ds[s, i:i + 1, :] = ext[f][r:r + 1, :]
        for k in range(3):
            ds[s, 13 + k:14 + k, :] = vxs[1, 4 + cy(k):5 + cy(k), :]
            ds[s, 16 + k:17 + k, :] = vys[1, 4 + cx(k):5 + cx(k), :]

    def slot(u):
        return ((lane + 4) % TZ) // 8 == u

    packs = {}
    for f in ALONG_Z:
        packs[f] = []
        for odd in (0, 1):
            packed = jnp.zeros((GROUP, TZ), F32)
            for u in range(16):
                g = MAIN_GROUPS[2 * u + odd]
                value = ext[f][g * 8:g * 8 + 8, :]
                if f == "c":
                    value = jnp.where(lane == TZ - 4, roll_lanes(vzm[g * 8:g * 8 + 8, :], -3), value)
                packed = jnp.where(slot(u), roll_lanes(value, 8 * u), packed)
            packs[f].append(packed)
    packed = jnp.zeros((GROUP, TZ), F32)
    for u in range(4):
        value = (vxs, vys)[u // 2][1, 4 + 8 * (u % 2):12 + 8 * (u % 2), :]
        packed = jnp.where(slot(u), roll_lanes(value, 8 * u), packed)
    lower = lane % 8 < 4
    for i, f in enumerate(ALONG_Z):
        one, two = packs[f]
        zs[0, i] = jnp.where(lower, one, roll_lanes(two, 4))
        zs[1, i] = jnp.where(lower, roll_lanes(one, 4), roll_lanes(two, 8))
        zown[2 * i] = one
        zown[2 * i + 1] = two
    zs[0, 4] = packed
    zs[1, 4] = packed
    zown[8] = packed

    def copies(sems, buffers):
        return [
            pltpu.make_async_remote_copy(
                src_ref=src, dst_ref=dst, send_sem=sems[0].at[i], recv_sem=sems[1].at[i],
                device_id=at_side(*side), device_id_type=MESH)
            for i, (side, (src, dst)) in enumerate(zip(SIDES, buffers))
        ]

    firsts = copies((ss, rs), [
        (a.at[s, pl.ds(0, 192 + 16 * s)], b.at[s, pl.ds(0, 192 + 16 * s)]) for a, b in ((xs, xr), (ys, yr)) for s in (0, 1)
    ] + [(ds.at[s], dr.at[s]) for s in range(4)])
    to_z = [
        pltpu.make_async_remote_copy(
            src_ref=zs.at[s], dst_ref=zr.at[s], send_sem=zss.at[s], recv_sem=zrs.at[s],
            device_id={"gz": iz + (2 * s - 1)}, device_id_type=MESH)
        for s in (0, 1)
    ]
    from_z = (jnp.logical_not(high_z), jnp.logical_not(low_z))
    pl.semaphore_wait(barrier, expected)

    @pl.when(bridge)
    def _():
        pl.semaphore_signal(met, inc=1, device_id=across, device_id_type=MESH)

    for s in (0, 1):
        @pl.when(from_z[1 - s])
        def _(s=s):
            to_z[s].start()
    for side, copy in zip(SIDES, firsts):
        @pl.when(has(*side))
        def _(copy=copy):
            copy.start()

    for d in range(OWN):
        cells = cell_r[d:d + 1, :]
        span = slice(d * CAP, (d + 1) * CAP)
        one = jnp.where(iota((ROWS, 1), 0) == cells // TZ, 1.0, 0.0).astype(BF)
        cone[0:ROWS, span] = one
        cone[ROWS:2 * ROWS, span] = one
        zsel[:, span] = jnp.where(iota((TZ, 1), 0) == cells % TZ, 1.0, 0.0).astype(F32)

    eye = iota((TONES, TONES), 0) == iota((TONES, TONES), 1)
    freq = jnp.sum(jnp.where(eye, tone_r[...], 0.0), axis=1, keepdims=True)
    freq = jnp.concatenate([freq, freq], axis=0)
    angle = freq * lane.astype(F32)
    basis = half_wave(angle, jnp.where(iota((NB, 1), 0) < TONES, 0.5, 0.0).astype(F32)) * 0.125
    for n in range(STEPS):
        bt[n * NB:(n + 1) * NB, :] = jnp.broadcast_to(basis[:, HIST + n:HIST + n + 1], (NB, CAP))
    held = iota((OWN, OWN), 0) == iota((OWN, OWN), 1)
    counts = jnp.sum(jnp.where(held, count_r[...].astype(F32), 0.0), axis=1, keepdims=True)
    live = jnp.where(lane.astype(F32) < counts, 1.0, 0.0).astype(F32)
    bt_out = pltpu.make_async_copy(bt, bt_h, osem.at[3])
    bt_out.start()

    @pl.when(bridge)
    def _():
        pl.semaphore_wait(met, 1)
        for mate in mates:
            pl.semaphore_signal(all_in, inc=1, device_id=mate, device_id_type=MESH)

    for i in range(4):
        sx, sy = SIDES[i]

        @pl.when(has(-sx, -sy))
        def _(i=i):
            along_x, s = i < 2, i % 2
            out = outer(s)
            firsts[i].wait_recv()
            got = (xr if along_x else yr).at[s]
            for j, (f, k) in enumerate(PLANES):
                ext[f][plane_at(along_x, out(k)), :] = got[j * 16:(j + 1) * 16, :]
            beside, through = (vys, vxs) if along_x else (vxs, vys)
            ends = got[160:176, :]
            for k in range(3):
                vzm[plane_at(along_x, out(k)), :] = pltpu.roll(ends, TZ - 1 - k, 1)
                beside[1, 4 + out(k):5 + out(k), :] = got[176 + k:177 + k, :]
            if s == 1:
                through[0, 4:20, :] = got[192:208, :]

    for i in range(4, 8):
        sx, sy = SIDES[i]

        @pl.when(has(-sx, -sy))
        def _(i=i, sx=sx, sy=sy):
            ox, oy = outer(up(sx)), outer(up(sy))
            firsts[i].wait_recv()
            for j, (f, a, b) in enumerate(CORNER):
                r = row_of(ox(a), oy(b))
                ext[f][r:r + 1, :] = dr[i - 4, j:j + 1, :]
            for k in range(3):
                if sx > 0:
                    vxs[0, 4 + oy(k):5 + oy(k), :] = dr[i - 4, 13 + k:14 + k, :]
                if sy > 0:
                    vys[0, 4 + ox(k):5 + ox(k), :] = dr[i - 4, 16 + k:17 + k, :]

    def borders(change, vx, vy):
        for k, x in ((0, 0), (1, TX)):
            r = row_of(x, -4)
            change[r:r + WIDE, :] = change[r:r + WIDE, :] + vx[k]
        for k, y in ((0, 0), (1, TY)):
            r = pl.ds(row_of(-4, y), WIDE, stride=WIDE)
            change[r, :] = change[r, :] + vy[k]

    def mirrors(refs, widths):
        for flag, low, along_x in (
            (low_x, True, True), (high_x, False, True), (low_y, True, False), (high_y, False, False)
        ):
            @pl.when(flag)
            def _(low=low, along_x=along_x):
                def rows(q):
                    return pl.ds(row_of(q, -4), WIDE) if along_x else pl.ds(row_of(-4, q), WIDE, stride=WIDE)

                for f, width in widths:
                    for k in range(width):
                        if low:
                            refs[f][rows(-1 - k), :] = refs[f][rows(k), :]
                        elif k == 0:
                            refs[f][rows(TX), :] = jnp.zeros((WIDE, TZ), F32)
                        else:
                            refs[f][rows(TX + k), :] = -refs[f][rows(TX - k), :]

    borders(cm, vxs, vys)
    mirrors(ext, WIDTHS + (("v", 3),))

    for s in (0, 1):
        @pl.when(from_z[s])
        def _(s=s):
            to_z[s].wait_recv()

    place = (lane + 4) % 8

    def joined(own, from_low, from_high, skip):
        below = jnp.zeros((GROUP, TZ), F32)
        above = jnp.zeros((GROUP, TZ), F32)
        for k in range(4):
            if not (skip and k == 3):
                below = jnp.where(place == 3 - k, roll_lanes(own, -(2 * k + 1)), below)
            if k:
                above = jnp.where(place == 4 + k, -roll_lanes(own, 2 * k), above)
        return jnp.where(
            place < 4, jnp.where(low_z, below, from_low), jnp.where(high_z, above, from_high))

    for i, f in enumerate(ALONG_Z):
        lows, highs = zr[1, i], zr[0, i]
        for odd in (0, 1):
            merged = joined(
                zown[2 * i + odd], roll_lanes(lows, -4 - 4 * odd), roll_lanes(highs, -4 * odd), f == "c")
            for u in range(16):
                g = MAIN_GROUPS[2 * u + odd]
                value = roll_lanes(merged, -8 * u)
                ring[f][g * 8:g * 8 + 8, :] = value
                if f == "c":
                    vzq[g * 8:g * 8 + 8, :] = roll_lanes(value, 3)
    merged = joined(zown[8], zr[1, 4], zr[0, 4], False)
    for u in range(4):
        (vxq, vyq)[u // 2][1, 4 + 8 * (u % 2):12 + 8 * (u % 2), :] = roll_lanes(merged, -8 * u)

    for face in range(4):
        along_x, s = face < 2, face % 2
        cell = inner(s)
        beside, through = (vyq, vxq) if along_x else (vxq, vyq)
        for k in range(3):
            spare[face, k:k + 1, :] = beside[1, 4 + cell(k):5 + cell(k), :]
        planes = [ring[f][plane_at(along_x, cell(k)), :] for f, k in RING_PLANES] + [spare[face]]
        if s == 1:
            planes.append(through[1, 4:20, :])
        packed = jnp.zeros((TY, TZ), F32)
        for u, value in enumerate(planes):
            packed = jnp.where(slot(u), roll_lanes(value, 8 * u), packed)
        qs[face] = packed
    for s, (sx, sy) in enumerate(DIAGS):
        cx, cy = inner(up(sx)), inner(up(sy))
        for i, (f, a, b) in enumerate(RING_CORNER):
            r = row_of(cx(a), cy(b))
            es[s, i:i + 1, :] = ring[f][r:r + 1, :]
        for k in range(2):
            es[s, 8 + k:9 + k, :] = vxq[1, 4 + cy(k):5 + cy(k), :]
            es[s, 10 + k:11 + k, :] = vyq[1, 4 + cx(k):5 + cx(k), :]
    seconds = copies((qss, qrs), [(qs.at[s], qr.at[s]) for s in range(4)] + [(es.at[s], er.at[s]) for s in range(4)])
    for side, copy in zip(SIDES, seconds):
        @pl.when(has(*side))
        def _(copy=copy):
            copy.start()

    for i in range(4):
        sx, sy = SIDES[i]

        @pl.when(has(-sx, -sy))
        def _(i=i):
            along_x, s = i < 2, i % 2
            out = outer(s)
            seconds[i].wait_recv()
            got = qr[i]
            for u, (f, k) in enumerate(RING_PLANES):
                ring[f][plane_at(along_x, out(k)), :] = roll_lanes(got, -8 * u)
            beside, through = (vyq, vxq) if along_x else (vxq, vyq)
            last = len(RING_PLANES)
            side_rows = roll_lanes(got, -8 * last)
            for k in range(3):
                beside[1, 4 + out(k):5 + out(k), :] = side_rows[k:k + 1, :]
            if s == 1:
                through[0, 4:20, :] = roll_lanes(got, -8 * (last + 1))

    for i in range(4, 8):
        sx, sy = SIDES[i]

        @pl.when(has(-sx, -sy))
        def _(i=i, sx=sx, sy=sy):
            ox, oy = outer(up(sx)), outer(up(sy))
            seconds[i].wait_recv()
            for j, (f, a, b) in enumerate(RING_CORNER):
                r = row_of(ox(a), oy(b))
                ring[f][r:r + 1, :] = er[i - 4, j:j + 1, :]
            for k in range(2):
                if sx > 0:
                    vxq[0, 4 + oy(k):5 + oy(k), :] = er[i - 4, 8 + k:9 + k, :]
                if sy > 0:
                    vyq[0, 4 + ox(k):5 + ox(k), :] = er[i - 4, 10 + k:11 + k, :]

    borders(cq, vxq, vyq)
    mirrors(ring, RING_WIDTHS)

    for g in range(4, 69):
        at = slice(g * 8, g * 8 + 8)
        cm[at, :] = cm[at, :] + roll_lanes(jnp.where(lane == TZ - 1, vzq[at, :], 0.0), 1)
        if 7 <= g < 66:
            flow = roll_lanes(jnp.where(lane == TZ - 1, vzm[at, :], 0.0), 1)
            cq[at, :] = cq[at, :] + jnp.where(high_z, 0.0, flow)

    for n in range(STEPS):
        d_main = (cm, d2m, d3m, d4)[n]
        d_ring = (cq, d2q, d3q, None)[n]
        main_span = (range(4, 69), range(7, 66), range(10, 63), [g for g in range(13, 60) if g % 3])[n]
        ring_span = (range(7, 66), range(10, 63), range(13, 60), ())[n]
        for g in main_span:
            at = slice(g * 8, g * 8 + 8)
            here, ghost = pm[n, at, :], pq[n, at, :]

            def stepped(ref, d, here, other):
                sums = (ref[n, g * 8 - WIDE:g * 8 - WIDE + 8, :] + ref[n, g * 8 + WIDE:g * 8 + WIDE + 8, :]) + (
                    ref[n, g * 8 - 1:g * 8 + 7, :] + ref[n, g * 8 + 1:g * 8 + 9, :])
                back = pltpu.roll(jnp.where(lane == TZ - 1, other, here), 1, 1)
                fore = pltpu.roll(jnp.where(lane == 0, other, here), TZ - 1, 1)
                new = d + 0.25 * (sums + (back + fore))
                return new if n == 0 else new + (0.5 * here - ref[n - 1, at, :])

            if n < STEPS - 1:
                pm[n + 1, at, :] = stepped(pm, d_main[at, :], here, ghost)
                if g in ring_span:
                    pq[n + 1, at, :] = stepped(pq, d_ring[at, :], ghost, here)
            else:
                x, half = divmod(g - 13, 3)
                own = slice(x * TY + half * 8, x * TY + half * 8 + 8)
                plast[own, :] = stepped(pm, d4[own, :], here, ghost)
        new = plast[...] if n == STEPS - 1 else jnp.concatenate(
            [pm[n + 1, row_of(x, 0):row_of(x, 0) + TY, :] for x in range(TX)], axis=0)
        both[n * TZ:(n + 1) * TZ, :] = jnp.concatenate(split(new.T), axis=1)

    for d in range(0, OWN, 2):
        span = slice(d * CAP, (d + 2) * CAP)
        seen = dot_nn(both[...], cone[:, span])
        for n in range(STEPS):
            got = jnp.sum(seen[n * TZ:(n + 1) * TZ, :] * zsel[:, span], axis=0, keepdims=True)
            sb[d * 8 + n:d * 8 + n + 1, :] = got[:, :CAP]
            sb[(d + 1) * 8 + n:(d + 1) * 8 + n + 1, :] = got[:, CAP:]

    def block_copy(k):
        target = lax.rem(iz + k, OWN)
        return pltpu.make_async_remote_copy(
            src_ref=sb.at[pl.ds(pl.multiple_of(target * 8, 8), 8)],
            dst_ref=rb.at[pl.ds(pl.multiple_of(iz * 8, 8), 8)],
            send_sem=ass.at[k], recv_sem=ars.at[k], device_id={"gz": target}, device_id_type=MESH)

    @pl.when(jnp.logical_not(bridge))
    def _():
        pl.semaphore_wait(all_in, 1)

    sends = [block_copy(k) for k in range(1, OWN)]
    for k in (8, 7, 9, 6, 10, 5, 11, 4, 12, 3, 13, 2, 14, 1, 15):
        sends[k - 1].start()
    mine = pl.ds(pl.multiple_of(iz * 8, 8), 8)
    rb[mine, :] = sb[mine, :]

    outs = [pltpu.make_async_copy(plast, fout_h.at[0], osem.at[0])]
    outs[0].start()
    for side, one, two in zip(SIDES, firsts, seconds):
        @pl.when(has(*side))
        def _(one=one, two=two):
            one.wait_send()
            two.wait_send()
    for s in (0, 1):
        @pl.when(from_z[1 - s])
        def _(s=s):
            to_z[s].wait_send()
    for g in range(13, 64):
        at = slice(g * 8, g * 8 + 8)
        sm[at, :] = (pm[0, at, :] + pm[1, at, :]) + (pm[2, at, :] + pm[3, at, :])
        sq[at, :] = (pq[0, at, :] + pq[1, at, :]) + (pq[2, at, :] + pq[3, at, :])
    for x in range(TX):
        at = slice(x * TY, (x + 1) * TY)
        r = row_of(x, 0)
        own = sm[r:r + TY, :]
        fv[1, at, :] = fv[1, at, :] - 0.5 * (sm[r + WIDE:r + WIDE + TY, :] - own)
        fv[2, at, :] = fv[2, at, :] - 0.5 * (sm[r + 1:r + 1 + TY, :] - own)
        fore = pltpu.roll(jnp.where(lane == 0, sq[r:r + TY, :], own), TZ - 1, 1)
        fv[3, at, :] = fv[3, at, :] - 0.5 * (fore - own)
    outs.append(pltpu.make_async_copy(fv.at[pl.ds(1, 3)], fout_h.at[pl.ds(1, 3)], osem.at[1]))
    outs[1].start()

    hist_load.wait()
    hv[HIST * OWN:, :] = jnp.zeros((STEPS * OWN, CAP), F32)
    bh, bl = split(basis)
    lhs = jnp.concatenate([bh, bl, bh], axis=1)
    for e in range(0, OWN, 2):
        hh, hl = split(jnp.concatenate(
            [hv[pl.ds(e, HIST + STEPS, stride=OWN), :], hv[pl.ds(e + 1, HIST + STEPS, stride=OWN), :]], axis=1))
        part = dot_nn(lhs, jnp.concatenate([hh, hh, hl], axis=0))
        ov[pl.ds(e, NB, stride=OWN), :] = part[:, :CAP] * live[e:e + 1]
        ov[pl.ds(e + 1, NB, stride=OWN), :] = part[:, CAP:] * live[e + 1:e + 2]
    ov_out = pltpu.make_async_copy(ov, cout_h, osem.at[2])
    ov_out.start()

    for copy in sends:
        copy.wait_recv()
    for n in range(STEPS):
        hb[n * OWN:(n + 1) * OWN, :] = rb[pl.ds(n, OWN, stride=8), :] * live
    outs.append(pltpu.make_async_copy(hb, heard_h, osem.at[4]))
    outs[-1].start()
    for copy in sends:
        copy.wait_send()
    for copy in outs + [bt_out, ov_out]:
        copy.wait()


PARTS = 4
PER = NB // PARTS


def finish(fields_h, part_h, heard_h, bt_h, fout_h, cout_h, fv, ov, hb, bt, sems, fsems):
    pieces = [pl.ds(k * PER * OWN, PER * OWN) for k in range(PARTS)]
    first = [pltpu.make_async_copy(heard_h, hb, sems.at[0]), pltpu.make_async_copy(bt_h, bt, sems.at[1])]
    loads = [pltpu.make_async_copy(part_h.at[r], ov.at[r], sems.at[2 + k]) for k, r in enumerate(pieces)]
    stores = [pltpu.make_async_copy(ov.at[r], cout_h.at[r], sems.at[2 + PARTS + k]) for k, r in enumerate(pieces)]
    gets = [pltpu.make_async_copy(fields_h.at[k], fv.at[k], fsems.at[k]) for k in range(4)]
    puts = [pltpu.make_async_copy(fv.at[k], fout_h.at[k], fsems.at[4 + k]) for k in range(4)]
    for copy in first + loads + gets:
        copy.start()
    for copy in first:
        copy.wait()
    heard = [hb[n * OWN:(n + 1) * OWN, :] for n in range(STEPS)]
    for k in range(PARTS):
        loads[k].wait()
        for j in range(k * PER, (k + 1) * PER):
            at = slice(j * OWN, (j + 1) * OWN)
            term = ov[at, :]
            for n in range(STEPS):
                term = term + bt[n * NB + j:n * NB + j + 1, :] * heard[n]
            ov[at, :] = term
        stores[k].start()
        gets[k].wait()
        puts[k].start()
    for copy in stores + puts:
        copy.wait()


def body(
    fields, tone_freq, mode_freq, mode_amp, mode_map, src_pos, src_id, src_gain, sample_cell, sample_count, history
):
    hbm = pl.BlockSpec(memory_space=pl.ANY)
    made = pl.pallas_call(
        kernel,
        out_shape=(
            jax.ShapeDtypeStruct((4, ROWS, TZ), F32),
            jax.ShapeDtypeStruct((NB * OWN, CAP), F32),
            jax.ShapeDtypeStruct((STEPS * OWN, CAP), F32),
            jax.ShapeDtypeStruct((STEPS * NB, CAP), F32),
        ),
        in_specs=[hbm] * 11,
        out_specs=(hbm,) * 4,
        scratch_shapes=[
            pltpu.VMEM((1, TONES), F32),
            pltpu.VMEM((1, MODES), F32),
            pltpu.VMEM((1, MODES), F32),
            pltpu.VMEM((1, MODES), jnp.int32),
            pltpu.VMEM((3, SRC), jnp.int32),
            pltpu.VMEM((1, SRC), jnp.int32),
            pltpu.VMEM((1, SRC), F32),
            pltpu.VMEM((OWN, CAP), jnp.int32),
            pltpu.VMEM((1, OWN), jnp.int32),
            pltpu.VMEM((4, ROWS, TZ), F32),
            pltpu.VMEM(((HIST + STEPS) * OWN, CAP), F32),
            pltpu.VMEM((STEPS, EXT, TZ), F32),
            pltpu.VMEM((STEPS, EXT, TZ), F32),
            pltpu.VMEM((EXT, TZ), F32),
            pltpu.VMEM((EXT, TZ), F32),
            pltpu.VMEM((EXT, TZ), F32),
            pltpu.VMEM((EXT, TZ), F32),
            pltpu.VMEM((EXT, TZ), F32),
            pltpu.VMEM((EXT, TZ), F32),
            pltpu.VMEM((ROWS, TZ), F32),
            pltpu.VMEM((EXT, TZ), F32),
            pltpu.VMEM((EXT, TZ), F32),
            pltpu.VMEM((2, WIDE, TZ), F32),
            pltpu.VMEM((2, WIDE, TZ), F32),
            pltpu.VMEM((2, WIDE, TZ), F32),
            pltpu.VMEM((2, WIDE, TZ), F32),
            pltpu.VMEM((ROWS, TZ), F32),
            pltpu.VMEM((EXT, TZ), F32),
            pltpu.VMEM((EXT, TZ), F32),
            pltpu.VMEM((8, 2048), F32),
            pltpu.VMEM((8, SRC), F32),
            pltpu.VMEM((1, SRC), F32),
            pltpu.VMEM((1, SRC), F32),
            pltpu.VMEM((ROWS, 2 * STEPS * TZ), F32),
            pltpu.VMEM((2 * ROWS, SLOTS), BF),
            pltpu.VMEM((TZ, SLOTS), F32),
            pltpu.VMEM((STEPS * TZ, 2 * ROWS), BF),
            pltpu.VMEM((NB * OWN, CAP), F32),
            pltpu.VMEM((STEPS * NB, CAP), F32),
            pltpu.VMEM((OWN * 8, CAP), F32),
            pltpu.VMEM((OWN * 8, CAP), F32),
            pltpu.VMEM((STEPS * OWN, CAP), F32),
            pltpu.VMEM((2, 208, TZ), F32),
            pltpu.VMEM((2, 208, TZ), F32),
            pltpu.VMEM((2, 208, TZ), F32),
            pltpu.VMEM((2, 208, TZ), F32),
            pltpu.VMEM((4, 24, TZ), F32),
            pltpu.VMEM((4, 24, TZ), F32),
            pltpu.VMEM((2, 5, GROUP, TZ), F32),
            pltpu.VMEM((2, 5, GROUP, TZ), F32),
            pltpu.VMEM((4, TY, TZ), F32),
            pltpu.VMEM((4, TY, TZ), F32),
            pltpu.VMEM((4, TY, TZ), F32),
            pltpu.VMEM((4, TY, TZ), F32),
            pltpu.VMEM((4, TY, TZ), F32),
            pltpu.VMEM((9, GROUP, TZ), F32),
            pltpu.SemaphoreType.DMA((9,)),
            pltpu.SemaphoreType.DMA((4,)),
            pltpu.SemaphoreType.DMA,
            pltpu.SemaphoreType.DMA((5,)),
            pltpu.SemaphoreType.DMA((8,)),
            pltpu.SemaphoreType.DMA((8,)),
            pltpu.SemaphoreType.DMA((2,)),
            pltpu.SemaphoreType.DMA((2,)),
            pltpu.SemaphoreType.DMA((8,)),
            pltpu.SemaphoreType.DMA((8,)),
            pltpu.SemaphoreType.DMA((OWN,)),
            pltpu.SemaphoreType.DMA((OWN,)),
            pltpu.SemaphoreType.REGULAR,
            pltpu.SemaphoreType.REGULAR,
        ],
        compiler_params=pltpu.CompilerParams(
            collective_id=0, has_side_effects=True, vmem_limit_bytes=63 * 1024 * 1024
        ),
    )(
        fields.reshape(4, ROWS, TZ),
        tone_freq.reshape(1, TONES),
        mode_freq.reshape(1, MODES),
        mode_amp.reshape(1, MODES),
        mode_map.reshape(1, MODES),
        src_pos,
        src_id.reshape(1, SRC),
        src_gain.reshape(1, SRC),
        sample_cell.reshape(OWN, CAP),
        sample_count.reshape(1, OWN),
        history.reshape(HIST * OWN, CAP),
    )
    fields_out, coefficients = pl.pallas_call(
        finish,
        out_shape=(
            jax.ShapeDtypeStruct((4, ROWS, TZ), F32),
            jax.ShapeDtypeStruct((NB * OWN, CAP), F32),
        ),
        in_specs=[hbm] * 4,
        out_specs=(hbm,) * 2,
        scratch_shapes=[
            pltpu.VMEM((4, ROWS, TZ), F32),
            pltpu.VMEM((NB * OWN, CAP), F32),
            pltpu.VMEM((STEPS * OWN, CAP), F32),
            pltpu.VMEM((STEPS * NB, CAP), F32),
            pltpu.SemaphoreType.DMA((2 + 2 * PARTS,)),
            pltpu.SemaphoreType.DMA((8,)),
        ],
        compiler_params=pltpu.CompilerParams(vmem_limit_bytes=63 * 1024 * 1024),
    )(*made)
    return fields_out.reshape(fields.shape), coefficients.reshape(NB, 1, 1, 1, OWN, CAP)


def solution(mesh):
    in_specs = (
        P(None, "gx", "gy", "gz"),
        P(),
        P(),
        P(),
        P(),
        P(),
        P(),
        P(),
        P("gx", "gy", "gz", None, None),
        P("gx", "gy", None, "gz"),
        P(None, "gx", "gy", "gz", None, None),
    )
    out_specs = (P(None, "gx", "gy", "gz"), P(None, "gx", "gy", "gz", None, None))
    return jax.shard_map(body, mesh=mesh, in_specs=in_specs, out_specs=out_specs, check_vma=False)
```

time: 36 us -> 34.7 us (0.964)
  local copies, waits for them, and re-layouts: 2.82 us -> 0 us
  Pallas kernels: 32.4 us -> 33.9 us
    unnamed x4 -> x0, local copies, waits for them, and re-layouts: 2.82 us -> none
    pallas_call x0 -> x1, Pallas kernels: none -> 2.35 us  [body(): pl.pallas_call(finish, out_shape=(jax.ShapeDtypeStruct((4, ROWS, TZ), F32...]
    pallas_call x1, Pallas kernels: 32.4 us -> 31.6 us  [body(): pl.pallas_call(kernel, out_shape=(jax.ShapeDtypeStruct((4, ROWS, TZ), F32...]
where the time goes in v4:
time: 34.7 us; the launch traced here: 34.5 us
  Pallas kernels  33.9 us (98%)
  between operations  0.64 us (2%)
    pallas_call x1, Pallas kernels, body(): pl.pallas_call(kernel, out_shape=(jax.ShapeDtypeStruct((4, ROWS, TZ), F32...  31.6 us
    pallas_call x1, Pallas kernels, body(): pl.pallas_call(finish, out_shape=(jax.ShapeDtypeStruct((4, ROWS, TZ), F32...  2.35 us

profile of v4, /device:TPU:1, one launch (start us, length us, event | category | flops | bytes accessed | tf_op | source)
XLA Modules:
  0.0 34.5 jit_solution(10323734013560103699)
XLA Ops:
  0.6 31.6 %shard_map.122 = (f32[4,256,128]{2,1,0:T(8,128)}, f32[1536,128]{1,0:T(8,128)}, f32[64,128]{1,0:T(8,128)}, f32[384,128]{1,0:T(8,128)}) custom-call(f32[4,256,128]{2,1,0:T(8,128)} %bitcast.15, f32[1,48]{1,0:T(1,128)} %bitcast.22, f32[1,2000]{1,0:T(1,128)} %bitcast.18, f32[1,2000]{1,0:T(1,128)} %bitcast.19, s32[1,2000]{1,0:T(1,128)} %bitcast.20, ...), custom_call_target="tpu_custom_call" | custom-call | tf_op jit(solution)/shard_map/pallas_call | solution.py:661
  32.2 2.3 %shard_map.123 = (f32[4,256,128]{2,1,0:T(8,128)}, f32[1536,128]{1,0:T(8,128)}) custom-call(f32[4,256,128]{2,1,0:T(8,128)} %get-tuple-element.8.fields_h, f32[1536,128]{1,0:T(8,128)} %get-tuple-element.9.part_h, f32[64,128]{1,0:T(8,128)} %get-tuple-element.10.heard_h, f32[384,128]{1,0:T(8,128)} %get-tuple-element.11.bt_h), custom_call_target="tpu_custom_call" | custom-call | tf_op jit(solution)/shard_map/pallas_call | solution.py:759

commit v5 on v4

--- a/solution.py
+++ b/solution.py
@@ -64,15 +64,16 @@
 WIDE = 24
 EXT = 584
 WIDTHS = (("p", 4), ("c", 3), ("d2", 2), ("d3", 1))
-PLANES = [(f, k) for f, width in WIDTHS for k in range(width)]
+LATER = [(f, k) for f, width in WIDTHS[1:] for k in range(width)]
 RING_WIDTHS = (("p", 3), ("c", 2), ("d2", 1), ("v", 3))
 RING_PLANES = [(f, k) for f, width in RING_WIDTHS for k in range(width)]
 DIAGS = ((-1, -1), (-1, 1), (1, -1), (1, 1))
 SIDES = ((-1, 0), (1, 0), (0, -1), (0, 1)) + DIAGS
-CORNER = [("p", i, j) for i in range(3) for j in range(3 - i)] + [
-    (f, i, j) for f in ("c", "v") for i in range(2) for j in range(2 - i)] + [("d2", 0, 0)]
+CORNER = [("p", i, j) for i in range(3) for j in range(3 - i)] + [("v", i, j) for i in range(2) for j in range(2 - i)]
+LATER_CORNER = [("c", i, j) for i in range(2) for j in range(2 - i)] + [("d2", 0, 0)]
 RING_CORNER = [(f, i, j) for f in ("p", "v") for i in range(2) for j in range(2 - i)] + [("c", 0, 0)]
 ALONG_Z = ("p", "c", "d2", "d3")
+Z_SLOT = {"p": 0, "c": 2, "d2": 3, "d3": 4}
 MAIN_GROUPS = [g for g in range(13, 60) if g % 3]
 
 
@@ -194,32 +195,17 @@
         a = jnp.where(iota((ROWS, 1), 0).astype(F32).astype(BF) == srow[:, span].astype(BF), ONE, ZERO)
         m = iota((TZ, 1), 0).astype(F32).astype(BF) == scol[:, span].astype(BF)
         b = jnp.concatenate([jnp.where(m, wv[q:q + 1, span].astype(BF), ZERO) for q in range(2 * STEPS)], axis=0)
-        return dot_nt(a, b)
+        return dot_nt(b, a)
 
     acc[...] = scattered(pl.ds(0, KC))
-
-    @pl.loop(1, SRC // KC)
-    def _(chunk):
-        acc[...] += scattered(pl.ds(pl.multiple_of(chunk * KC, KC), KC))
 
     for copy in loads:
         copy.wait()
     for x in range(TX):
         at = slice(x * TY, (x + 1) * TY)
         to = slice(row_of(x, 0), row_of(x, 0) + TY)
-        added = [acc[at, n * TZ:(n + 1) * TZ] + acc[at, (STEPS + n) * TZ:(STEPS + n + 1) * TZ] for n in range(STEPS)]
-        p = fv[0, at, :]
-        vx, vy, vz = (fv[k, at, :] for k in (1, 2, 3))
-        gone = vx + (vy - jnp.where(sub == 0, 0.0, pltpu.roll(vy, 1, 0)))
-        gone = gone + (vz - jnp.where(lane == 0, 0.0, pltpu.roll(vz, 1, 1)))
-        if x:
-            gone = gone - fv[1, (x - 1) * TY:x * TY, :]
-        pm[0, to, :] = p
-        cm[to, :] = added[0] - 0.5 * (gone + p)
-        d2m[to, :] = added[1] - added[0]
-        d3m[to, :] = added[2] - added[1]
-        d4[at, :] = added[3] - added[2]
-        vzm[to, :] = 0.5 * vz
+        pm[0, to, :] = fv[0, at, :]
+        vzm[to, :] = 0.5 * fv[3, at, :]
     vxs[1, 4:20, :] = 0.5 * fv[1, ROWS - TY:ROWS, :]
     vys[1, 4:20, :] = 0.5 * fv[2, pl.ds(TY - 1, TX, stride=TY), :]
 
@@ -239,32 +225,33 @@
         along_x, s = face < 2, face % 2
         cell = inner(s)
         to = (xs if along_x else ys).at[s]
-        for i, (f, k) in enumerate(PLANES):
-            to[i * 16:(i + 1) * 16, :] = ext[f][plane_at(along_x, cell(k)), :]
+        for k in range(4):
+            to[k * 16:(k + 1) * 16, :] = ext["p"][plane_at(along_x, cell(k)), :]
         ends = jnp.zeros((TY, TZ), F32)
         for k in range(3):
             ends = jnp.where(lane == k, pltpu.roll(vzm[plane_at(along_x, cell(k)), :], k + 1, 1), ends)
-        to[160:176, :] = ends
+        to[64:80, :] = ends
         beside, through = (vys, vxs) if along_x else (vxs, vys)
         for k in range(3):
-            to[176 + k:177 + k, :] = beside[1, 4 + cell(k):5 + cell(k), :]
+            to[80 + k:81 + k, :] = beside[1, 4 + cell(k):5 + cell(k), :]
         if s == 1:
-            to[192:208, :] = through[1, 4:20, :]
+            to[96:112, :] = through[1, 4:20, :]
     for s, (sx, sy) in enumerate(DIAGS):
         cx, cy = inner(up(sx)), inner(up(sy))
         for i, (f, a, b) in enumerate(CORNER):
             r = row_of(cx(a), cy(b))
             ds[s, i:i + 1, :] = ext[f][r:r + 1, :]
         for k in range(3):
-            ds[s, 13 + k:14 + k, :] = vxs[1, 4 + cy(k):5 + cy(k), :]
-            ds[s, 16 + k:17 + k, :] = vys[1, 4 + cx(k):5 + cx(k), :]
+            ds[s, 9 + k:10 + k, :] = vxs[1, 4 + cy(k):5 + cy(k), :]
+            ds[s, 12 + k:13 + k, :] = vys[1, 4 + cx(k):5 + cx(k), :]
 
     def slot(u):
         return ((lane + 4) % TZ) // 8 == u
 
-    packs = {}
-    for f in ALONG_Z:
-        packs[f] = []
+    lower = lane % 8 < 4
+
+    def pack_z(f):
+        made = []
         for odd in (0, 1):
             packed = jnp.zeros((GROUP, TZ), F32)
             for u in range(16):
@@ -273,54 +260,102 @@
                 if f == "c":
                     value = jnp.where(lane == TZ - 4, roll_lanes(vzm[g * 8:g * 8 + 8, :], -3), value)
                 packed = jnp.where(slot(u), roll_lanes(value, 8 * u), packed)
-            packs[f].append(packed)
+            made.append(packed)
+        one, two = made
+        i = Z_SLOT[f]
+        zs[0, i] = jnp.where(lower, one, roll_lanes(two, 4))
+        zs[1, i] = jnp.where(lower, roll_lanes(one, 4), roll_lanes(two, 8))
+        zown[2 * i] = one
+        zown[2 * i + 1] = two
+
+    pack_z("p")
     packed = jnp.zeros((GROUP, TZ), F32)
     for u in range(4):
         value = (vxs, vys)[u // 2][1, 4 + 8 * (u % 2):12 + 8 * (u % 2), :]
         packed = jnp.where(slot(u), roll_lanes(value, 8 * u), packed)
-    lower = lane % 8 < 4
-    for i, f in enumerate(ALONG_Z):
-        one, two = packs[f]
-        zs[0, i] = jnp.where(lower, one, roll_lanes(two, 4))
-        zs[1, i] = jnp.where(lower, roll_lanes(one, 4), roll_lanes(two, 8))
-        zown[2 * i] = one
-        zown[2 * i + 1] = two
-    zs[0, 4] = packed
-    zs[1, 4] = packed
-    zown[8] = packed
-
-    def copies(sems, buffers):
+    zs[0, 1] = packed
+    zs[1, 1] = packed
+    zown[2] = packed
+
+    def copies(sends, arrivals, buffers):
         return [
             pltpu.make_async_remote_copy(
-                src_ref=src, dst_ref=dst, send_sem=sems[0].at[i], recv_sem=sems[1].at[i],
+                src_ref=src, dst_ref=dst, send_sem=sends.at[i], recv_sem=arrivals.at[i],
                 device_id=at_side(*side), device_id_type=MESH)
             for i, (side, (src, dst)) in enumerate(zip(SIDES, buffers))
         ]
 
-    firsts = copies((ss, rs), [
-        (a.at[s, pl.ds(0, 192 + 16 * s)], b.at[s, pl.ds(0, 192 + 16 * s)]) for a, b in ((xs, xr), (ys, yr)) for s in (0, 1)
-    ] + [(ds.at[s], dr.at[s]) for s in range(4)])
-    to_z = [
-        pltpu.make_async_remote_copy(
-            src_ref=zs.at[s], dst_ref=zr.at[s], send_sem=zss.at[s], recv_sem=zrs.at[s],
-            device_id={"gz": iz + (2 * s - 1)}, device_id_type=MESH)
-        for s in (0, 1)
-    ]
+    def first_copies(t):
+        faces = [(a.at[s, r], b.at[s, r]) for a, b in ((xs, xr), (ys, yr)) for s, r in (
+            (0, pl.ds(112, 96) if t else pl.ds(0, 96)), (1, pl.ds(112, 96) if t else pl.ds(0, 112)))]
+        r = pl.ds(16, 8) if t else pl.ds(0, 16)
+        return copies(ss.at[t], rs.at[t], faces + [(ds.at[s, r], dr.at[s, r]) for s in range(4)])
+
+    def z_copies(t):
+        r = pl.ds(2, 3) if t else pl.ds(0, 2)
+        return [
+            pltpu.make_async_remote_copy(
+                src_ref=zs.at[s, r], dst_ref=zr.at[s, r], send_sem=zss.at[t, s], recv_sem=zrs.at[t, s],
+                device_id={"gz": iz + (2 * s - 1)}, device_id_type=MESH)
+            for s in (0, 1)
+        ]
+
+    firsts = [first_copies(t) for t in (0, 1)]
+    to_z = [z_copies(t) for t in (0, 1)]
     from_z = (jnp.logical_not(high_z), jnp.logical_not(low_z))
+
+    def send_first(t):
+        for s in (0, 1):
+            @pl.when(from_z[1 - s])
+            def _(s=s):
+                to_z[t][s].start()
+        for side, copy in zip(SIDES, firsts[t]):
+            @pl.when(has(*side))
+            def _(copy=copy):
+                copy.start()
+
     pl.semaphore_wait(barrier, expected)
 
     @pl.when(bridge)
     def _():
         pl.semaphore_signal(met, inc=1, device_id=across, device_id_type=MESH)
 
-    for s in (0, 1):
-        @pl.when(from_z[1 - s])
-        def _(s=s):
-            to_z[s].start()
-    for side, copy in zip(SIDES, firsts):
-        @pl.when(has(*side))
-        def _(copy=copy):
-            copy.start()
+    send_first(0)
+
+    @pl.loop(1, SRC // KC)
+    def _(chunk):
+        acc[...] += scattered(pl.ds(pl.multiple_of(chunk * KC, KC), KC))
+
+    sheets = [(acc[n * TZ:(n + 1) * TZ, :] + acc[(STEPS + n) * TZ:(STEPS + n + 1) * TZ, :]).T for n in range(STEPS)]
+    for x in range(TX):
+        at = slice(x * TY, (x + 1) * TY)
+        to = slice(row_of(x, 0), row_of(x, 0) + TY)
+        added = [sheet[at, :] for sheet in sheets]
+        p = fv[0, at, :]
+        vx, vy, vz = (fv[k, at, :] for k in (1, 2, 3))
+        gone = vx + (vy - jnp.where(sub == 0, 0.0, pltpu.roll(vy, 1, 0)))
+        gone = gone + (vz - jnp.where(lane == 0, 0.0, pltpu.roll(vz, 1, 1)))
+        if x:
+            gone = gone - fv[1, (x - 1) * TY:x * TY, :]
+        cm[to, :] = added[0] - 0.5 * (gone + p)
+        d2m[to, :] = added[1] - added[0]
+        d3m[to, :] = added[2] - added[1]
+        d4[at, :] = added[3] - added[2]
+
+    for face in range(4):
+        along_x, s = face < 2, face % 2
+        cell = inner(s)
+        to = (xs if along_x else ys).at[s]
+        for i, (f, k) in enumerate(LATER):
+            to[112 + i * 16:128 + i * 16, :] = ext[f][plane_at(along_x, cell(k)), :]
+    for s, (sx, sy) in enumerate(DIAGS):
+        cx, cy = inner(up(sx)), inner(up(sy))
+        for i, (f, a, b) in enumerate(LATER_CORNER):
+            r = row_of(cx(a), cy(b))
+            ds[s, 16 + i:17 + i, :] = ext[f][r:r + 1, :]
+    for f in ALONG_Z[1:]:
+        pack_z(f)
+    send_first(1)
 
     for d in range(OWN):
         cells = cell_r[d:d + 1, :]
@@ -356,17 +391,17 @@
         def _(i=i):
             along_x, s = i < 2, i % 2
             out = outer(s)
-            firsts[i].wait_recv()
+            firsts[0][i].wait_recv()
             got = (xr if along_x else yr).at[s]
-            for j, (f, k) in enumerate(PLANES):
-                ext[f][plane_at(along_x, out(k)), :] = got[j * 16:(j + 1) * 16, :]
+            for k in range(4):
+                ext["p"][plane_at(along_x, out(k)), :] = got[k * 16:(k + 1) * 16, :]
             beside, through = (vys, vxs) if along_x else (vxs, vys)
-            ends = got[160:176, :]
+            ends = got[64:80, :]
             for k in range(3):
                 vzm[plane_at(along_x, out(k)), :] = pltpu.roll(ends, TZ - 1 - k, 1)
-                beside[1, 4 + out(k):5 + out(k), :] = got[176 + k:177 + k, :]
+                beside[1, 4 + out(k):5 + out(k), :] = got[80 + k:81 + k, :]
             if s == 1:
-                through[0, 4:20, :] = got[192:208, :]
+                through[0, 4:20, :] = got[96:112, :]
 
     for i in range(4, 8):
         sx, sy = SIDES[i]
@@ -374,15 +409,38 @@
         @pl.when(has(-sx, -sy))
         def _(i=i, sx=sx, sy=sy):
             ox, oy = outer(up(sx)), outer(up(sy))
-            firsts[i].wait_recv()
+            firsts[0][i].wait_recv()
             for j, (f, a, b) in enumerate(CORNER):
                 r = row_of(ox(a), oy(b))
                 ext[f][r:r + 1, :] = dr[i - 4, j:j + 1, :]
             for k in range(3):
                 if sx > 0:
-                    vxs[0, 4 + oy(k):5 + oy(k), :] = dr[i - 4, 13 + k:14 + k, :]
+                    vxs[0, 4 + oy(k):5 + oy(k), :] = dr[i - 4, 9 + k:10 + k, :]
                 if sy > 0:
-                    vys[0, 4 + ox(k):5 + ox(k), :] = dr[i - 4, 16 + k:17 + k, :]
+                    vys[0, 4 + ox(k):5 + ox(k), :] = dr[i - 4, 12 + k:13 + k, :]
+
+    for i in range(4):
+        sx, sy = SIDES[i]
+
+        @pl.when(has(-sx, -sy))
+        def _(i=i):
+            along_x, s = i < 2, i % 2
+            out = outer(s)
+            firsts[1][i].wait_recv()
+            got = (xr if along_x else yr).at[s]
+            for j, (f, k) in enumerate(LATER):
+                ext[f][plane_at(along_x, out(k)), :] = got[112 + j * 16:128 + j * 16, :]
+
+    for i in range(4, 8):
+        sx, sy = SIDES[i]
+
+        @pl.when(has(-sx, -sy))
+        def _(i=i, sx=sx, sy=sy):
+            ox, oy = outer(up(sx)), outer(up(sy))
+            firsts[1][i].wait_recv()
+            for j, (f, a, b) in enumerate(LATER_CORNER):
+                r = row_of(ox(a), oy(b))
+                ext[f][r:r + 1, :] = dr[i - 4, 16 + j:17 + j, :]
 
     def borders(change, vx, vy):
         for k, x in ((0, 0), (1, TX)):
@@ -416,7 +474,8 @@
     for s in (0, 1):
         @pl.when(from_z[s])
         def _(s=s):
-            to_z[s].wait_recv()
+            to_z[0][s].wait_recv()
+            to_z[1][s].wait_recv()
 
     place = (lane + 4) % 8
 
@@ -431,7 +490,8 @@
         return jnp.where(
             place < 4, jnp.where(low_z, below, from_low), jnp.where(high_z, above, from_high))
 
-    for i, f in enumerate(ALONG_Z):
+    for f in ALONG_Z:
+        i = Z_SLOT[f]
         lows, highs = zr[1, i], zr[0, i]
         for odd in (0, 1):
             merged = joined(
@@ -442,7 +502,7 @@
                 ring[f][g * 8:g * 8 + 8, :] = value
                 if f == "c":
                     vzq[g * 8:g * 8 + 8, :] = roll_lanes(value, 3)
-    merged = joined(zown[8], zr[1, 4], zr[0, 4], False)
+    merged = joined(zown[2], zr[1, 1], zr[0, 1], False)
     for u in range(4):
         (vxq, vyq)[u // 2][1, 4 + 8 * (u % 2):12 + 8 * (u % 2), :] = roll_lanes(merged, -8 * u)
 
@@ -467,7 +527,7 @@
         for k in range(2):
             es[s, 8 + k:9 + k, :] = vxq[1, 4 + cy(k):5 + cy(k), :]
             es[s, 10 + k:11 + k, :] = vyq[1, 4 + cx(k):5 + cx(k), :]
-    seconds = copies((qss, qrs), [(qs.at[s], qr.at[s]) for s in range(4)] + [(es.at[s], er.at[s]) for s in range(4)])
+    seconds = copies(qss, qrs, [(qs.at[s], qr.at[s]) for s in range(4)] + [(es.at[s], er.at[s]) for s in range(4)])
     for side, copy in zip(SIDES, seconds):
         @pl.when(has(*side))
         def _(copy=copy):
@@ -574,15 +634,16 @@
 
     outs = [pltpu.make_async_copy(plast, fout_h.at[0], osem.at[0])]
     outs[0].start()
-    for side, one, two in zip(SIDES, firsts, seconds):
+    for side, *three in zip(SIDES, *firsts, seconds):
         @pl.when(has(*side))
-        def _(one=one, two=two):
-            one.wait_send()
-            two.wait_send()
+        def _(three=three):
+            for copy in three:
+                copy.wait_send()
     for s in (0, 1):
         @pl.when(from_z[1 - s])
         def _(s=s):
-            to_z[s].wait_send()
+            to_z[0][s].wait_send()
+            to_z[1][s].wait_send()
     for g in range(13, 64):
         at = slice(g * 8, g * 8 + 8)
         sm[at, :] = (pm[0, at, :] + pm[1, at, :]) + (pm[2, at, :] + pm[3, at, :])
@@ -702,7 +763,7 @@
             pltpu.VMEM((8, SRC), F32),
             pltpu.VMEM((1, SRC), F32),
             pltpu.VMEM((1, SRC), F32),
-            pltpu.VMEM((ROWS, 2 * STEPS * TZ), F32),
+            pltpu.VMEM((2 * STEPS * TZ, ROWS), F32),
             pltpu.VMEM((2 * ROWS, SLOTS), BF),
             pltpu.VMEM((TZ, SLOTS), F32),
             pltpu.VMEM((STEPS * TZ, 2 * ROWS), BF),
@@ -724,15 +785,15 @@
             pltpu.VMEM((4, TY, TZ), F32),
             pltpu.VMEM((4, TY, TZ), F32),
             pltpu.VMEM((4, TY, TZ), F32),
-            pltpu.VMEM((9, GROUP, TZ), F32),
+            pltpu.VMEM((10, GROUP, TZ), F32),
             pltpu.SemaphoreType.DMA((9,)),
             pltpu.SemaphoreType.DMA((4,)),
             pltpu.SemaphoreType.DMA,
             pltpu.SemaphoreType.DMA((5,)),
-            pltpu.SemaphoreType.DMA((8,)),
-            pltpu.SemaphoreType.DMA((8,)),
-            pltpu.SemaphoreType.DMA((2,)),
-            pltpu.SemaphoreType.DMA((2,)),
+            pltpu.SemaphoreType.DMA((2, 8)),
+            pltpu.SemaphoreType.DMA((2, 8)),
+            pltpu.SemaphoreType.DMA((2, 2)),
+            pltpu.SemaphoreType.DMA((2, 2)),
             pltpu.SemaphoreType.DMA((8,)),
             pltpu.SemaphoreType.DMA((8,)),
             pltpu.SemaphoreType.DMA((OWN,)),

time: 34.7 us -> 33.7 us (0.971)
  Pallas kernels: 33.9 us -> 32.9 us
    pallas_call x1, Pallas kernels: 31.6 us -> 30.6 us  [body(): pl.pallas_call(kernel, out_shape=(jax.ShapeDtypeStruct((4, ROWS, TZ), F32...]
where the time goes in v5:
time: 33.7 us; the launch traced here: 33.5 us
  Pallas kernels  32.9 us (98%)
  between operations  0.64 us (2%)
    pallas_call x1, Pallas kernels, body(): pl.pallas_call(kernel, out_shape=(jax.ShapeDtypeStruct((4, ROWS, TZ), F32...  30.6 us
    pallas_call x1, Pallas kernels, body(): pl.pallas_call(finish, out_shape=(jax.ShapeDtypeStruct((4, ROWS, TZ), F32...  2.35 us

profile of v5, /device:TPU:1, one launch (start us, length us, event | category | flops | bytes accessed | tf_op | source)
XLA Modules:
  0.0 33.5 jit_solution(6746148399660907145)
XLA Ops:
  0.6 30.6 %shard_map.122 = (f32[4,256,128]{2,1,0:T(8,128)}, f32[1536,128]{1,0:T(8,128)}, f32[64,128]{1,0:T(8,128)}, f32[384,128]{1,0:T(8,128)}) custom-call(f32[4,256,128]{2,1,0:T(8,128)} %bitcast.15, f32[1,48]{1,0:T(1,128)} %bitcast.22, f32[1,2000]{1,0:T(1,128)} %bitcast.18, f32[1,2000]{1,0:T(1,128)} %bitcast.19, s32[1,2000]{1,0:T(1,128)} %bitcast.20, ...), custom_call_target="tpu_custom_call" | custom-call | tf_op jit(solution)/shard_map/pallas_call | solution.py:722
  31.2 2.3 %shard_map.123 = (f32[4,256,128]{2,1,0:T(8,128)}, f32[1536,128]{1,0:T(8,128)}) custom-call(f32[4,256,128]{2,1,0:T(8,128)} %get-tuple-element.8.fields_h, f32[1536,128]{1,0:T(8,128)} %get-tuple-element.9.part_h, f32[64,128]{1,0:T(8,128)} %get-tuple-element.10.heard_h, f32[384,128]{1,0:T(8,128)} %get-tuple-element.11.bt_h), custom_call_target="tpu_custom_call" | custom-call | tf_op jit(solution)/shard_map/pallas_call | solution.py:820

commit v6 on v5

--- a/solution.py
+++ b/solution.py
@@ -101,47 +101,6 @@
     low_y, high_y = iy == 0, iy == 3
     low_z, high_z = iz == 0, iz == OWN - 1
 
-    def has(sx, sy):
-        ok = None
-        for s, low, high in ((sx, low_x, high_x), (sy, low_y, high_y)):
-            if s:
-                here = jnp.logical_not(low if s < 0 else high)
-                ok = here if ok is None else ok & here
-        return ok
-
-    def at_side(sx, sy):
-        where = {}
-        if sx:
-            where["gx"] = ix + sx
-        if sy:
-            where["gy"] = iy + sy
-        return where
-
-    barrier = pltpu.get_barrier_semaphore()
-    half = (iz // HALF) * HALF
-    bridge = (iz == BRIDGE) | (iz == BRIDGE + HALF)
-    border = (iz == HALF - 1) | (iz == HALF)
-    across = {"gz": lax.rem(iz + HALF, OWN)}
-    mates = [{"gz": half + lax.rem(iz - half + k, HALF)} for k in range(1, HALF)]
-
-    @pl.when(border)
-    def _():
-        pl.semaphore_signal(barrier, inc=1, device_id={"gz": OWN - 1 - iz}, device_id_type=MESH)
-
-    @pl.when(bridge)
-    def _():
-        pl.semaphore_signal(barrier, inc=1, device_id=across, device_id_type=MESH)
-
-    for mate in mates:
-        pl.semaphore_signal(barrier, inc=1, device_id=mate, device_id_type=MESH)
-    expected = HALF - 1 + jnp.where(border, 1, 0) + jnp.where(bridge, 1, 0)
-    for side in SIDES:
-        expected = expected + jnp.where(has(*side), 1, 0)
-
-        @pl.when(has(*side))
-        def _(side=side):
-            pl.semaphore_signal(barrier, inc=1, device_id=at_side(*side), device_id_type=MESH)
-
     small = [
         pltpu.make_async_copy(src, dst, isem.at[k])
         for k, (src, dst) in enumerate((
@@ -153,6 +112,47 @@
     loads = [pltpu.make_async_copy(fields_h.at[k], fv.at[k], fsem.at[k]) for k in range(4)]
     for copy in loads:
         copy.start()
+    def has(sx, sy):
+        ok = None
+        for s, low, high in ((sx, low_x, high_x), (sy, low_y, high_y)):
+            if s:
+                here = jnp.logical_not(low if s < 0 else high)
+                ok = here if ok is None else ok & here
+        return ok
+
+    def at_side(sx, sy):
+        where = {}
+        if sx:
+            where["gx"] = ix + sx
+        if sy:
+            where["gy"] = iy + sy
+        return where
+
+    barrier = pltpu.get_barrier_semaphore()
+    half = (iz // HALF) * HALF
+    bridge = (iz == BRIDGE) | (iz == BRIDGE + HALF)
+    border = (iz == HALF - 1) | (iz == HALF)
+    across = {"gz": lax.rem(iz + HALF, OWN)}
+    mates = [{"gz": half + lax.rem(iz - half + k, HALF)} for k in range(1, HALF)]
+
+    @pl.when(border)
+    def _():
+        pl.semaphore_signal(barrier, inc=1, device_id={"gz": OWN - 1 - iz}, device_id_type=MESH)
+
+    @pl.when(bridge)
+    def _():
+        pl.semaphore_signal(barrier, inc=1, device_id=across, device_id_type=MESH)
+
+    for mate in mates:
+        pl.semaphore_signal(barrier, inc=1, device_id=mate, device_id_type=MESH)
+    expected = HALF - 1 + jnp.where(border, 1, 0) + jnp.where(bridge, 1, 0)
+    for side in SIDES:
+        expected = expected + jnp.where(has(*side), 1, 0)
+
+        @pl.when(has(*side))
+        def _(side=side):
+            pl.semaphore_signal(barrier, inc=1, device_id=at_side(*side), device_id_type=MESH)
+
     hist_load = pltpu.make_async_copy(hist_h, hv.at[pl.ds(0, HIST * OWN)], hsem)
     hist_load.start()
 
@@ -161,7 +161,7 @@
     row8 = iota((8, 1), 0)
     ext = {"p": pm.at[0], "c": cm, "v": vzm, "d2": d2m, "d3": d3m}
     ring = {"p": pq.at[0], "c": cq, "d2": d2q, "d3": d3q, "v": vzq}
-    for ref in (vxs, vys, vxq, vyq, spare, sb):
+    for ref in (vxs, vys, vxq, vyq, spare):
         ref[...] = jnp.zeros_like(ref)
 
     ms[...] = jnp.zeros_like(ms)
@@ -314,13 +314,12 @@
             def _(copy=copy):
                 copy.start()
 
-    pl.semaphore_wait(barrier, expected)
-
-    @pl.when(bridge)
+    slow = border | bridge
+
+    @pl.when(jnp.logical_not(slow))
     def _():
-        pl.semaphore_signal(met, inc=1, device_id=across, device_id_type=MESH)
-
-    send_first(0)
+        pl.semaphore_wait(barrier, expected)
+        send_first(0)
 
     @pl.loop(1, SRC // KC)
     def _(chunk):
@@ -355,6 +354,17 @@
             ds[s, 16 + i:17 + i, :] = ext[f][r:r + 1, :]
     for f in ALONG_Z[1:]:
         pack_z(f)
+
+    @pl.when(slow)
+    def _():
+        pl.semaphore_wait(barrier, expected)
+
+        @pl.when(bridge)
+        def _():
+            pl.semaphore_signal(met, inc=1, device_id=across, device_id_type=MESH)
+
+        send_first(0)
+
     send_first(1)
 
     for d in range(OWN):
@@ -607,20 +617,23 @@
             [pm[n + 1, row_of(x, 0):row_of(x, 0) + TY, :] for x in range(TX)], axis=0)
         both[n * TZ:(n + 1) * TZ, :] = jnp.concatenate(split(new.T), axis=1)
 
-    for d in range(0, OWN, 2):
-        span = slice(d * CAP, (d + 2) * CAP)
-        seen = dot_nn(both[...], cone[:, span])
-        for n in range(STEPS):
-            got = jnp.sum(seen[n * TZ:(n + 1) * TZ, :] * zsel[:, span], axis=0, keepdims=True)
-            sb[d * 8 + n:d * 8 + n + 1, :] = got[:, :CAP]
-            sb[(d + 1) * 8 + n:(d + 1) * 8 + n + 1, :] = got[:, CAP:]
+        if n >= 2:
+            first = 0 if n == 2 else 3
+            for d in range(0, OWN, 2):
+                span = slice(d * CAP, (d + 2) * CAP)
+                seen = dot_nn(both[first * TZ:(n + 1) * TZ, :], cone[:, span])
+                for m in range(first, n + 1):
+                    part = seen[(m - first) * TZ:(m - first + 1) * TZ, :]
+                    got = jnp.sum(part * zsel[:, span], axis=0, keepdims=True)
+                    sb[d, m:m + 1, :] = got[:, :CAP]
+                    sb[d + 1, m:m + 1, :] = got[:, CAP:]
 
     def block_copy(k):
         target = lax.rem(iz + k, OWN)
         return pltpu.make_async_remote_copy(
-            src_ref=sb.at[pl.ds(pl.multiple_of(target * 8, 8), 8)],
-            dst_ref=rb.at[pl.ds(pl.multiple_of(iz * 8, 8), 8)],
-            send_sem=ass.at[k], recv_sem=ars.at[k], device_id={"gz": target}, device_id_type=MESH)
+            src_ref=sb.at[target],
+            dst_ref=rb.at[iz],
+            send_sem=ass, recv_sem=ars, device_id={"gz": target}, device_id_type=MESH)
 
     @pl.when(jnp.logical_not(bridge))
     def _():
@@ -629,8 +642,7 @@
     sends = [block_copy(k) for k in range(1, OWN)]
     for k in (8, 7, 9, 6, 10, 5, 11, 4, 12, 3, 13, 2, 14, 1, 15):
         sends[k - 1].start()
-    mine = pl.ds(pl.multiple_of(iz * 8, 8), 8)
-    rb[mine, :] = sb[mine, :]
+    rb[iz] = sb[iz]
 
     outs = [pltpu.make_async_copy(plast, fout_h.at[0], osem.at[0])]
     outs[0].start()
@@ -672,14 +684,16 @@
     ov_out = pltpu.make_async_copy(ov, cout_h, osem.at[2])
     ov_out.start()
 
-    for copy in sends:
-        copy.wait_recv()
+    every = pltpu.make_async_remote_copy(
+        src_ref=sb.at[pl.ds(0, OWN - 1)], dst_ref=rb.at[pl.ds(0, OWN - 1)], send_sem=ass, recv_sem=ars,
+        device_id={"gz": lax.rem(iz + 1, OWN)}, device_id_type=MESH)
+    every.wait_recv()
     for n in range(STEPS):
-        hb[n * OWN:(n + 1) * OWN, :] = rb[pl.ds(n, OWN, stride=8), :] * live
+        for e in range(OWN):
+            hb[n * OWN + e:n * OWN + e + 1, :] = rb[e, n:n + 1, :] * live[e:e + 1, :]
     outs.append(pltpu.make_async_copy(hb, heard_h, osem.at[4]))
     outs[-1].start()
-    for copy in sends:
-        copy.wait_send()
+    every.wait_send()
     for copy in outs + [bt_out, ov_out]:
         copy.wait()
 
@@ -769,8 +783,8 @@
             pltpu.VMEM((STEPS * TZ, 2 * ROWS), BF),
             pltpu.VMEM((NB * OWN, CAP), F32),
             pltpu.VMEM((STEPS * NB, CAP), F32),
-            pltpu.VMEM((OWN * 8, CAP), F32),
-            pltpu.VMEM((OWN * 8, CAP), F32),
+            pltpu.VMEM((OWN, STEPS, CAP), F32),
+            pltpu.VMEM((OWN, STEPS, CAP), F32),
             pltpu.VMEM((STEPS * OWN, CAP), F32),
             pltpu.VMEM((2, 208, TZ), F32),
             pltpu.VMEM((2, 208, TZ), F32),
@@ -796,8 +810,8 @@
             pltpu.SemaphoreType.DMA((2, 2)),
             pltpu.SemaphoreType.DMA((8,)),
             pltpu.SemaphoreType.DMA((8,)),
-            pltpu.SemaphoreType.DMA((OWN,)),
-            pltpu.SemaphoreType.DMA((OWN,)),
+            pltpu.SemaphoreType.DMA,
+            pltpu.SemaphoreType.DMA,
             pltpu.SemaphoreType.REGULAR,
             pltpu.SemaphoreType.REGULAR,
         ],

time: 33.7 us -> 33.1 us (0.982)
  Pallas kernels: 32.9 us -> 32.3 us
    pallas_call x1, Pallas kernels: 30.6 us -> 30 us  [body(): pl.pallas_call(kernel, out_shape=(jax.ShapeDtypeStruct((4, ROWS, TZ), F32...]
where the time goes in v6:
time: 33.1 us; the launch traced here: 32.9 us
  Pallas kernels  32.3 us (98%)
  between operations  0.64 us (2%)
    pallas_call x1, Pallas kernels, body(): pl.pallas_call(kernel, out_shape=(jax.ShapeDtypeStruct((4, ROWS, TZ), F32...  30 us
    pallas_call x1, Pallas kernels, body(): pl.pallas_call(finish, out_shape=(jax.ShapeDtypeStruct((4, ROWS, TZ), F32...  2.35 us

profile of v6, /device:TPU:1, one launch (start us, length us, event | category | flops | bytes accessed | tf_op | source)
XLA Modules:
  0.0 32.9 jit_solution(1731417440134320239)
XLA Ops:
  0.6 30.0 %shard_map.122 = (f32[4,256,128]{2,1,0:T(8,128)}, f32[1536,128]{1,0:T(8,128)}, f32[64,128]{1,0:T(8,128)}, f32[384,128]{1,0:T(8,128)}) custom-call(f32[4,256,128]{2,1,0:T(8,128)} %bitcast.15, f32[1,48]{1,0:T(1,128)} %bitcast.22, f32[1,2000]{1,0:T(1,128)} %bitcast.18, f32[1,2000]{1,0:T(1,128)} %bitcast.19, s32[1,2000]{1,0:T(1,128)} %bitcast.20, ...), custom_call_target="tpu_custom_call" | custom-call | tf_op jit(solution)/shard_map/pallas_call | solution.py:736
  30.6 2.3 %shard_map.123 = (f32[4,256,128]{2,1,0:T(8,128)}, f32[1536,128]{1,0:T(8,128)}) custom-call(f32[4,256,128]{2,1,0:T(8,128)} %get-tuple-element.8.fields_h, f32[1536,128]{1,0:T(8,128)} %get-tuple-element.9.part_h, f32[64,128]{1,0:T(8,128)} %get-tuple-element.10.heard_h, f32[384,128]{1,0:T(8,128)} %get-tuple-element.11.bt_h), custom_call_target="tpu_custom_call" | custom-call | tf_op jit(solution)/shard_map/pallas_call | solution.py:834

commit v7 on v6

--- a/solution.py
+++ b/solution.py
@@ -197,8 +197,6 @@
         b = jnp.concatenate([jnp.where(m, wv[q:q + 1, span].astype(BF), ZERO) for q in range(2 * STEPS)], axis=0)
         return dot_nt(b, a)
 
-    acc[...] = scattered(pl.ds(0, KC))
-
     for copy in loads:
         copy.wait()
     for x in range(TX):
@@ -320,6 +318,8 @@
     def _():
         pl.semaphore_wait(barrier, expected)
         send_first(0)
+
+    acc[...] = scattered(pl.ds(0, KC))
 
     @pl.loop(1, SRC // KC)
     def _(chunk):

time: 33.1 us -> 33.3 us (level)
  no operation moved by 1% of the time
where the time goes in v7:
time: 33.3 us; the launch traced here: 33.2 us
  Pallas kernels  32.5 us (98%)
  between operations  0.64 us (2%)
    pallas_call x1, Pallas kernels, body(): pl.pallas_call(kernel, out_shape=(jax.ShapeDtypeStruct((4, ROWS, TZ), F32...  30.2 us
    pallas_call x1, Pallas kernels, body(): pl.pallas_call(finish, out_shape=(jax.ShapeDtypeStruct((4, ROWS, TZ), F32...  2.35 us

profile of v7, /device:TPU:1, one launch (start us, length us, event | category | flops | bytes accessed | tf_op | source)
XLA Modules:
  0.0 33.2 jit_solution(17883789549684989846)
XLA Ops:
  0.6 30.2 %shard_map.122 = (f32[4,256,128]{2,1,0:T(8,128)}, f32[1536,128]{1,0:T(8,128)}, f32[64,128]{1,0:T(8,128)}, f32[384,128]{1,0:T(8,128)}) custom-call(f32[4,256,128]{2,1,0:T(8,128)} %bitcast.15, f32[1,48]{1,0:T(1,128)} %bitcast.22, f32[1,2000]{1,0:T(1,128)} %bitcast.18, f32[1,2000]{1,0:T(1,128)} %bitcast.19, s32[1,2000]{1,0:T(1,128)} %bitcast.20, ...), custom_call_target="tpu_custom_call" | custom-call | tf_op jit(solution)/shard_map/pallas_call | solution.py:736
  30.8 2.3 %shard_map.123 = (f32[4,256,128]{2,1,0:T(8,128)}, f32[1536,128]{1,0:T(8,128)}) custom-call(f32[4,256,128]{2,1,0:T(8,128)} %get-tuple-element.8.fields_h, f32[1536,128]{1,0:T(8,128)} %get-tuple-element.9.part_h, f32[64,128]{1,0:T(8,128)} %get-tuple-element.10.heard_h, f32[384,128]{1,0:T(8,128)} %get-tuple-element.11.bt_h), custom_call_target="tpu_custom_call" | custom-call | tf_op jit(solution)/shard_map/pallas_call | solution.py:834
